TPU v7x, 128 devices: a whole 4x4x4 slice. The times are simulated.
128 devices in a mesh: row: 8 (over x, core), col: 16 (over y, z).
Axes of the slice: x: 4, y: 4, z: 4, core: 2. Of those that a mesh axis runs over, the one named last changes fastest.
Arguments:
- latent: bfloat16 [384, 512, 640], P('row', 'col'), may hold values from -260 to 260
- blend: int32 [384, 512], P('row', 'col'), may hold values from 1 to 3
- gamma_local: float32 [640], replicated, may hold values from 0.5 to 1.5
- beta_local: float32 [640], replicated, may hold values from -3 to 3
- kernel_local: bfloat16 [3, 3, 640, 640], replicated, may hold values from -0.078125 to 0.078125
- bias_local: float32 [640], replicated, may hold values from -3 to 3
- gamma_dilated: float32 [640], replicated, may hold values from 0.5 to 1.5
- beta_dilated: float32 [640], replicated, may hold values from -3 to 3
- kernel_dilated: bfloat16 [3, 3, 640, 640], replicated, may hold values from -0.078125 to 0.078125
- bias_dilated: float32 [640], replicated, may hold values from -3 to 3
Outputs:
- blended: bfloat16 [384, 512, 640], P('row', 'col')
All inputs are finite; a program needn't handle non-finite values.
Results may differ from a plain program's by a relative error of at most 0.0052.
Values may be sent and summed in bfloat16 or wider, within the bound.
A program may use at most 192 MiB of HBM per device.

v0:
```python
import jax
import jax.numpy as jnp
from jax import lax
from jax.sharding import PartitionSpec as P

GROUPS = 32
STRIDE = 4


def extended(block, sides, width):
    for axis, dim in sides:
        count = lax.axis_size(axis)
        forward = [(i, i + 1) for i in range(count - 1)]
        backward = [(target, source) for source, target in forward]
        low = lax.ppermute(
            lax.slice_in_dim(block, block.shape[dim] - width, None, axis=dim), axis, forward
        )
        high = lax.ppermute(lax.slice_in_dim(block, 0, width, axis=dim), axis, backward)
        block = jnp.concatenate([low, block, high], axis=dim)
    return block


def apply_taps(padded, kernel, step, rows, cols):
    total = None
    for tap_row in range(3):
        for tap_col in range(3):
            piece = padded[
                ...,
                tap_row * step : tap_row * step + rows,
                tap_col * step : tap_col * step + cols,
                :,
            ]
            term = jnp.einsum(
                "...hwc,cd->...hwd",
                piece,
                kernel[tap_row, tap_col],
                preferred_element_type=jnp.float32,
            )
            total = term if total is None else total + term
    return total


def activate(
    block,
    mean_local,
    var_local,
    mean_sub,
    var_sub,
    gamma_local,
    beta_local,
    gamma_dilated,
    beta_dilated,
):
    values = block.astype(jnp.float32)
    height, width, chans = values.shape
    per_group = chans // GROUPS
    grouped = values.reshape(height, width, GROUPS, per_group)
    normed = ((grouped - mean_local[:, None]) * lax.rsqrt(var_local + 1e-05)[:, None]).reshape(
        height, width, chans
    )
    act_local = jax.nn.silu(normed * gamma_local + beta_local).astype(jnp.bfloat16)
    subs = values.reshape(height // STRIDE, STRIDE, width // STRIDE, STRIDE, GROUPS, per_group)
    normed_sub = (
        (subs - mean_sub[None, :, None, :, :, None])
        * lax.rsqrt(var_sub + 1e-05)[None, :, None, :, :, None]
    ).reshape(height, width, chans)
    act_dilated = jax.nn.silu(normed_sub * gamma_dilated + beta_dilated).astype(jnp.bfloat16)
    return (act_local, act_dilated)


def per_device(
    latent,
    blend,
    gamma_local,
    beta_local,
    kernel_local,
    bias_local,
    gamma_dilated,
    beta_dilated,
    kernel_dilated,
    bias_dilated,
):
    x = latent.astype(jnp.float32)
    rows, cols, chans = x.shape
    per_group = chans // GROUPS
    cells = rows * lax.axis_size("row") * cols * lax.axis_size("col")
    count_local = float(cells * per_group)
    count_sub = float(cells * per_group // (STRIDE * STRIDE))
    grouped = x.reshape(rows, cols, GROUPS, per_group)
    subs = x.reshape(rows // STRIDE, STRIDE, cols // STRIDE, STRIDE, GROUPS, per_group)
    sum_local = jnp.sum(grouped, axis=(0, 1, 3))
    sum_sub = jnp.sum(subs, axis=(0, 2, 5))
    sum_local, sum_sub = lax.psum((sum_local, sum_sub), ("row", "col"))
    mean_local = sum_local / count_local
    mean_sub = sum_sub / count_sub
    centered = grouped - mean_local[:, None]
    centered_sub = subs - mean_sub[None, :, None, :, :, None]
    square_local = jnp.sum(centered * centered, axis=(0, 1, 3))
    square_sub = jnp.sum(centered_sub * centered_sub, axis=(0, 2, 5))
    square_local, square_sub = lax.psum((square_local, square_sub), ("row", "col"))
    var_local = square_local / count_local
    var_sub = square_sub / count_sub
    act_local, act_dilated = activate(
        latent,
        mean_local,
        var_local,
        mean_sub,
        var_sub,
        gamma_local,
        beta_local,
        gamma_dilated,
        beta_dilated,
    )
    padded_local = extended(act_local, (("row", 0), ("col", 1)), 1)
    local = apply_taps(padded_local, kernel_local, 1, rows, cols) + bias_local
    sub_rows = rows // STRIDE
    sub_cols = cols // STRIDE
    by_sub = act_dilated.reshape(sub_rows, STRIDE, sub_cols, STRIDE, chans).transpose(1, 3, 0, 2, 4)
    by_sub = by_sub.reshape(STRIDE * STRIDE, sub_rows, sub_cols, chans)
    collected = lax.all_to_all(by_sub, "col", split_axis=0, concat_axis=2, tiled=True)
    rimmed = extended(collected, (("row", 1),), 1)
    rimmed = jnp.pad(rimmed, ((0, 0), (0, 0), (1, 1), (0, 0)))
    full_cols = collected.shape[2]
    result = (apply_taps(rimmed, kernel_dilated, 1, sub_rows, full_cols) + bias_dilated).astype(
        jnp.bfloat16
    )
    returned = lax.all_to_all(result, "col", split_axis=2, concat_axis=0, tiled=True)
    returned = returned.reshape(STRIDE, STRIDE, sub_rows, sub_cols, chans).transpose(2, 0, 3, 1, 4)
    dilated = returned.reshape(rows, cols, chans)
    weight = blend.astype(jnp.float32)[:, :, None]
    mixed = (weight * local + (4.0 - weight) * dilated.astype(jnp.float32)) * 0.25
    return mixed.astype(jnp.bfloat16)


def solution(mesh):
    placed = (P("row", "col", None), P("row", "col"), P(), P(), P(), P(), P(), P(), P(), P())
    return jax.shard_map(
        per_device, mesh=mesh, in_specs=placed, out_specs=P("row", "col", None), check_vma=False
    )
```

profile of v0, /device:TPU:1, one launch (start us, length us, event | category | flops | bytes accessed | tf_op | source)
XLA Modules:
  0.0 422.7 jit_solution(13267373976805299193)
XLA Ops:
  0.0 32.0 %reshape.90 = f32[12,4,8,4,32,20]{5,4,3,2,1,0:T(8,128)} reshape(bf16[48,32,640]{2,1,0:T(8,128)(2,1)} %param.10) | data formatting | bytes 5898240 | tf_op jit(solution)/shard_map/reshape | solution.py:62
  32.5 9.8 %reduce_sum.56 = f32[4,4,32]{2,1,0:T(4,128)S(1)} reduce(f32[12,4,8,4,32,20]{5,4,3,2,1,0:T(8,128)} %reshape.90, f32[]{:T(128)} %constant.8.clone.1), dimensions={0,2,5}, to_apply=%region_6.0 | reduce | flops 982528 | bytes 3934212 | tf_op jit(solution)/shard_map/reduce_sum | solution.py:92
  42.4 68.9 %all-reduce.2 = (f32[4,4,32]{2,1,0:T(4,128)S(1)}, f32[32]{0:T(128)S(1)}) all-reduce(f32[4,4,32]{2,1,0:T(4,128)S(1)} %reduce_sum.56, f32[32]{0:T(128)S(1)} %reduce_sum.52), channel_id=1, replica_groups=mesh['row'=8,'col'=16] {'row','col'}, use_global_device_ids=true, to_apply=%region_7.0 | all-reduce | flops 544 | bytes 4352 | tf_op jit(solution)/shard_map/psum | solution.py:93
  111.3 10.4 %multiply_reduce_fusion = f32[4,4,32]{2,1,0:T(4,128)S(1)} fusion(f32[12,4,8,4,32,20]{5,4,3,2,1,0:T(8,128)} %reshape.90, f32[4,4,32]{2,1,0:T(4,128)S(1)} %broadcast_multiply_fusion), kind=kLoop, calls=%fused_computation | loop fusion | flops 2948608 | bytes 3936256 | tf_op jit(solution)/shard_map/reduce_sum | solution.py:99
  121.9 0.6 multiply_reduce_fusion.1
  122.7 62.9 %all-reduce.1 = (f32[4,4,32]{2,1,0:T(4,128)S(1)}, f32[32]{0:T(128)S(1)}) all-reduce(f32[4,4,32]{2,1,0:T(4,128)S(1)} %multiply_reduce_fusion, f32[32]{0:T(128)S(1)} %reduce_sum.55), channel_id=1, replica_groups=mesh['row'=8,'col'=16] {'row','col'}, use_global_device_ids=true, to_apply=%region_9.10 | all-reduce | flops 544 | bytes 4352 | tf_op jit(solution)/shard_map/psum | solution.py:100
  185.8 11.6 %mul.88 = f32[12,4,8,4,32,20]{5,4,3,2,1,0:T(8,128)} broadcast(f32[4,4,32]{2,1,0:T(4,128)S(1)} %add_rsqrt_fusion), dimensions={1,3,4} | broadcast | bytes 3934208 | tf_op jit(solution)/shard_map/mul | solution.py:64
  197.4 22.3 %mul.89 = f32[48,32,640]{2,1,0:T(8,128)} reshape(f32[12,4,8,4,32,20]{5,4,3,2,1,0:T(8,128)} %mul.88) | data formatting | bytes 7864320 | tf_op jit(solution)/shard_map/mul | solution.py:64
  219.7 11.6 %sub.48 = f32[12,4,8,4,32,20]{5,4,3,2,1,0:T(8,128)} broadcast(f32[4,4,32]{2,1,0:T(4,128)S(1)} %broadcast_multiply_fusion), dimensions={1,3,4} | broadcast | bytes 3934208 | tf_op jit(solution)/shard_map/sub | solution.py:64
  231.3 22.4 %sub.49 = f32[48,32,640]{2,1,0:T(8,128)} reshape(f32[12,4,8,4,32,20]{5,4,3,2,1,0:T(8,128)} %sub.48) | data formatting | bytes 7864320 | tf_op jit(solution)/shard_map/sub | solution.py:64
  253.7 6.1 %multiply_convert_fusion.2 = (bf16[48,32,640]{2,1,0:T(8,128)(2,1)}, bf16[48,32,640]{2,1,0:T(8,128)(2,1)}) fusion(bf16[48,32,640]{2,1,0:T(8,128)(2,1)S(1)} %copy-done, f32[640]{0:T(1024)S(1)} %copy-done.6, f32[640]{0:T(1024)S(1)} %copy-done.7, f32[640]{0:T(1024)S(1)} %mul.79, f32[640]{0:T(1024)S(1)} %sub.43, f32[640]{0:T(1024)S(1)} %copy-done.8, ...), kind=kLoop, calls=%fused_computation.7 | loop fusion | flops 18677760 | bytes 13777920 | tf_op jit(solution)/shard_map/convert_element_type | solution.py:61
  259.9 4.3 %reshape.91 = bf16[12,4,8,4,640]{4,3,2,1,0:T(4,128)(2,1)} reshape(bf16[48,32,640]{2,1,0:T(8,128)(2,1)} %get-tuple-element.16) | data formatting | bytes 3932160 | tf_op jit(solution)/shard_map/reshape | solution.py:118
  264.2 3.3 copy.29
  267.5 4.8 %all-to-all-start = ((bf16[16,12,8,640]{3,2,1,0:T(8,128)(2,1)}), bf16[16,12,8,640]{3,2,1,0:T(8,128)(2,1)}, u32[]{:S(2)}, u32[]{:S(2)}) async-start(bf16[16,12,8,640]{3,2,1,0:T(8,128)(2,1)} %bitcast.148), calls=%async_computation | async-start | bytes 3932160 | tf_op jit(solution)/shard_map/all_to_all | solution.py:120
  272.4 2.8 collective-permute-start.1
  275.2 2.7 collective-permute-start
  278.0 4.9 %fusion.59 = f32[48,32,640]{2,1,0:T(8,128)} fusion(bf16[48,32,640]{2,1,0:T(8,128)(2,1)S(1)} %copy-done.1, bf16[3,3,640,640]{3,2,1,0:T(8,128)(2,1)} %param.14), kind=kOutput, calls=%fused_computation.76 | convolution fusion | flops 1258291200 | bytes 6717440 | tf_op jit(solution)/shard_map/...hwc,cd->...hwd/dot_general | solution.py:33
  283.3 1.3 collective-permute-start.3
  284.6 4.1 collective-permute-start.2
  288.7 4.9 %fusion.10 = f32[48,32,640]{2,1,0:T(8,128)} fusion(bf16[1,32,640]{2,1,0:T(8,128)(2,1)S(1)} %collective-permute-done.1, bf16[48,32,640]{2,1,0:T(8,128)(2,1)S(1)} %copy-done.1, bf16[3,3,640,640]{3,2,1,0:T(8,128)(2,1)} %param.14), kind=kOutput, calls=%fused_computation.21 | convolution fusion | flops 1262305280 | bytes 6758400 | tf_op jit(solution)/shard_map/...hwc,cd->...hwd/dot_general | solution.py:33
  293.6 5.0 %fusion.6 = f32[48,32,640]{2,1,0:T(8,128)} fusion(bf16[48,32,640]{2,1,0:T(8,128)(2,1)S(1)} %copy-done.1, bf16[1,32,640]{2,1,0:T(8,128)(2,1)S(1)} %collective-permute-done, bf16[3,3,640,640]{3,2,1,0:T(8,128)(2,1)} %param.14), kind=kOutput, calls=%fused_computation.17 | convolution fusion | flops 1262305280 | bytes 6758400 | tf_op jit(solution)/shard_map/...hwc,cd->...hwd/dot_general | solution.py:33
  298.6 0.5 collective-permute-done.3
  299.1 4.5 %pad_maximum_fusion = (bf16[50,33,640]{2,1,0:T(8,128)(2,1)}, bf16[50,33,640]{2,1,0:T(8,128)(2,1)}) fusion(bf16[50,1,640]{2,1,0:T(2,128)(2,1)S(1)} %collective-permute-done.3, bf16[1,32,640]{2,1,0:T(8,128)(2,1)S(1)} %collective-permute-done.1, bf16[48,32,640]{2,1,0:T(8,128)(2,1)S(1)} %copy-done.1, bf16[1,32,640]{2,1,0:T(8,128)(2,1)S(1)} %collective-permute-done, ...), kind=kLoop, calls=%fused_computation.14 | loop fusion | flops 16896000 | bytes 6400000 | tf_op jit(solution)/shard_map/concatenate | solution.py:19
  303.6 1.9 copy_bitcast_fusion
  305.6 2.2 collective-permute-start.5
  307.8 3.6 collective-permute-start.4
  311.4 3.7 fusion.42
  315.2 1.9 fusion.5
  317.1 2.0 fusion.19
  319.1 3.8 fusion.20
  322.9 3.8 fusion.21
  326.7 3.9 fusion.22
  330.6 3.9 fusion.27
  334.5 3.8 fusion.16
  338.3 3.8 fusion.24
  342.1 9.5 %fusion.44 = bf16[1,12,128,640]{3,2,1,0:T(8,128)(2,1)S(1)} fusion(f32[640]{0:T(1024)S(1)} %copy-done.11, f32[12,128,640]{2,1,0:T(8,128)} %fusion.16, f32[12,128,640]{2,1,0:T(8,128)S(1)} %fusion.19, f32[12,128,640]{2,1,0:T(8,128)} %fusion.20, f32[12,128,640]{2,1,0:T(8,128)S(1)} %fusion.42, f32[12,128,640]{2,1,0:T(8,128)} %fusion.21, ...), kind=kOutput, calls=%fused_computation.60 | convolution fusion | flops 1268121600 | bytes 36212736 | tf_op jit(solution)/shard_map/...hwc,cd->...hwd/dot_general | solution.py:33
  351.6 2.7 copy.32
  354.3 8.3 %all-to-all-start.1 = ((bf16[1,12,128,640]{3,1,0,2:T(8,128)(2,1)}), bf16[1,12,128,640]{3,1,0,2:T(8,128)(2,1)S(1)}, u32[]{:S(2)}, u32[]{:S(2)}) async-start(bf16[1,12,128,640]{3,1,0,2:T(8,128)(2,1)} %copy.32), calls=%async_computation.1 | async-start | bytes 5242880 | tf_op jit(solution)/shard_map/all_to_all | solution.py:127
  362.6 5.7 %fusion.32 = f32[48,32,640]{2,1,0:T(8,128)} fusion(bf16[50,33,640]{2,1,0:T(8,128)(2,1)} %get-tuple-element.10, bf16[3,3,640,640]{3,2,1,0:T(8,128)(2,1)} %param.14), kind=kOutput, calls=%fused_computation.47 | convolution fusion | flops 1258291200 | bytes 6717440 | tf_op jit(solution)/shard_map/...hwc,cd->...hwd/dot_general | solution.py:33
  368.3 5.2 %fusion.36 = f32[48,32,640]{2,1,0:T(8,128)} fusion(bf16[50,33,640]{2,1,0:T(8,128)(2,1)S(1)} %copy-done.4, bf16[3,3,640,640]{3,2,1,0:T(8,128)(2,1)} %param.14), kind=kOutput, calls=%fused_computation.51 | convolution fusion | flops 1258291200 | bytes 6717440 | tf_op jit(solution)/shard_map/...hwc,cd->...hwd/dot_general | solution.py:33
  373.5 5.0 %fusion.34 = f32[48,32,640]{2,1,0:T(8,128)} fusion(bf16[50,33,640]{2,1,0:T(8,128)(2,1)S(1)} %copy-done.2, bf16[3,3,640,640]{3,2,1,0:T(8,128)(2,1)} %param.14), kind=kOutput, calls=%fused_computation.49 | convolution fusion | flops 1258291200 | bytes 6717440 | tf_op jit(solution)/shard_map/...hwc,cd->...hwd/dot_general | solution.py:33
  378.5 5.0 %fusion.38 = f32[48,32,640]{2,1,0:T(8,128)} fusion(bf16[50,33,640]{2,1,0:T(8,128)(2,1)S(1)} %copy-done.2, bf16[3,3,640,640]{3,2,1,0:T(8,128)(2,1)} %param.14), kind=kOutput, calls=%fused_computation.53 | convolution fusion | flops 1258291200 | bytes 6717440 | tf_op jit(solution)/shard_map/...hwc,cd->...hwd/dot_general | solution.py:33
  383.5 5.1 %fusion.40 = f32[48,32,640]{2,1,0:T(8,128)} fusion(bf16[50,33,640]{2,1,0:T(8,128)(2,1)S(1)} %copy-done.4, bf16[3,3,640,640]{3,2,1,0:T(8,128)(2,1)} %param.14), kind=kOutput, calls=%fused_computation.55 | convolution fusion | flops 1258291200 | bytes 6717440 | tf_op jit(solution)/shard_map/...hwc,cd->...hwd/dot_general | solution.py:33
  388.6 10.9 %all-to-all-done.1 = bf16[1,12,128,640]{3,1,0,2:T(8,128)(2,1)S(1)} async-done(((bf16[1,12,128,640]{3,1,0,2:T(8,128)(2,1)}), bf16[1,12,128,640]{3,1,0,2:T(8,128)(2,1)S(1)}, u32[]{:S(2)}, u32[]{:S(2)}) %all-to-all-start.1) | async-done | bytes 1966112 | tf_op jit(solution)/shard_map/all_to_all | solution.py:127
  399.5 0.4 bitcast_convert_fusion
  399.9 3.0 copy.35
  403.0 5.4 %reshape.102 = f32[48,32,640]{2,1,0:T(8,128)} reshape(f32[12,4,8,4,640]{4,3,2,1,0:T(4,128)} %copy.35) | data formatting | bytes 7864320 | tf_op jit(solution)/shard_map/convert_element_type | solution.py:131
  408.3 14.2 %multiply_convert_fusion = bf16[48,32,640]{2,1,0:T(8,128)(2,1)} fusion(f32[48,32,640]{2,1,0:T(8,128)} %reshape.102, f32[48,32,640]{2,1,0:T(8,128)} %fusion.10, f32[48,32,640]{2,1,0:T(8,128)} %fusion.32, f32[48,32,640]{2,1,0:T(8,128)} %fusion.34, f32[48,32,640]{2,1,0:T(8,128)} %fusion.59, f32[48,32,640]{2,1,0:T(8,128)} %fusion.36, ...), kind=kOutput, calls=%fused_computation.4 | convolution fusion | flops 1272053760 | bytes 40194048 | tf_op jit(solution)/shard_map/...hwc,cd->...hwd/dot_general | solution.py:33
  (55 shorter events, 1.6 us)
Async XLA Ops:
  0.0 32.0 %copy-start = (bf16[48,32,640]{2,1,0:T(8,128)(2,1)S(1)}, bf16[48,32,640]{2,1,0:T(8,128)(2,1)}, u32[]{:S(2)}) copy-start(bf16[48,32,640]{2,1,0:T(8,128)(2,1)} %param.10) | copy-start | bytes 5898244
  231.3 22.4 %copy-start.6 = (f32[640]{0:T(1024)S(1)}, f32[640]{0:T(1024)}, u32[]{:S(2)}) copy-start(f32[640]{0:T(1024)} %param.13) | copy-start | bytes 7684
  231.3 22.4 %copy-start.7 = (f32[640]{0:T(1024)S(1)}, f32[640]{0:T(1024)}, u32[]{:S(2)}) copy-start(f32[640]{0:T(1024)} %param.12) | copy-start | bytes 7684
  231.3 22.4 %copy-start.8 = (f32[640]{0:T(1024)S(1)}, f32[640]{0:T(1024)}, u32[]{:S(2)}) copy-start(f32[640]{0:T(1024)} %param.17) | copy-start | bytes 7684
  231.3 22.4 %copy-start.9 = (f32[640]{0:T(1024)S(1)}, f32[640]{0:T(1024)}, u32[]{:S(2)}) copy-start(f32[640]{0:T(1024)} %param.16) | copy-start | bytes 7684
  264.2 8.2 %copy-start.1 = (bf16[48,32,640]{2,1,0:T(8,128)(2,1)S(1)}, bf16[48,32,640]{2,1,0:T(8,128)(2,1)}, u32[]{:S(2)}) copy-start(bf16[48,32,640]{2,1,0:T(8,128)(2,1)} %get-tuple-element.15) | copy-start | bytes 5898244
  267.5 36.1 %all-to-all-start = ((bf16[16,12,8,640]{3,2,1,0:T(8,128)(2,1)}), bf16[16,12,8,640]{3,2,1,0:T(8,128)(2,1)}, u32[]{:S(2)}, u32[]{:S(2)}) async-start(bf16[16,12,8,640]{3,2,1,0:T(8,128)(2,1)} %bitcast.148), calls=%async_computation | async-start | bytes 3932160 | tf_op jit(solution)/shard_map/all_to_all | solution.py:120
  272.3 10.5 %copy-start.5 = (s32[48,32]{0,1:T(8,128)S(1)}, s32[48,32]{0,1:T(8,128)}, u32[]{:S(2)}) copy-start(s32[48,32]{0,1:T(8,128)} %param.11) | copy-start | bytes 18436
  272.4 10.7 %collective-permute-start.1 = (bf16[1,32,640]{2,1,0:T(8,128)(2,1)S(1)}, bf16[1,32,640]{2,1,0:T(8,128)(2,1)S(1)}, u32[]{:S(2)}, u32[]{:S(2)}) collective-permute-start(bf16[1,32,640]{2,1,0:T(8,128)(2,1)S(1)} %get-tuple-element.14), channel_id=1, source_target_pairs={{16,0},{32,16},{48,32},{64,48},{80,64},{96,80},{112,96},{17,1},{33... | collective-permute-start | bytes 122888 | tf_op jit(solution)/shard_map/ppermute | solution.py:18
  275.2 7.8 %collective-permute-start = (bf16[1,32,640]{2,1,0:T(8,128)(2,1)S(1)}, bf16[1,32,640]{2,1,0:T(8,128)(2,1)S(1)}, u32[]{:S(2)}, u32[]{:S(2)}) collective-permute-start(bf16[1,32,640]{2,1,0:T(8,128)(2,1)S(1)} %get-tuple-element.13), channel_id=1, source_target_pairs={{0,16},{16,32},{32,48},{48,64},{64,80},{80,96},{96,112},{1,17},{17... | collective-permute-start | bytes 122888 | tf_op jit(solution)/shard_map/ppermute | solution.py:15
  283.3 15.9 %collective-permute-start.3 = (bf16[50,1,640]{2,1,0:T(2,128)(2,1)S(1)}, bf16[50,1,640]{2,1,0:T(2,128)(2,1)S(1)}, u32[]{:S(2)}, u32[]{:S(2)}) collective-permute-start(bf16[50,1,640]{2,1,0:T(2,128)(2,1)S(1)} %get-tuple-element.11), channel_id=1, source_target_pairs={{1,0},{2,1},{3,2},{4,3},{5,4},{6,5},{7,6},{8,7},{9,8},{10,9},{11,1... | collective-permute-start | bytes 192008 | tf_op jit(solution)/shard_map/ppermute | solution.py:18
  284.6 14.6 %collective-permute-start.2 = (bf16[50,1,640]{2,1,0:T(2,128)(2,1)S(1)}, bf16[50,1,640]{2,1,0:T(2,128)(2,1)S(1)}, u32[]{:S(2)}, u32[]{:S(2)}) collective-permute-start(bf16[50,1,640]{2,1,0:T(2,128)(2,1)S(1)} %get-tuple-element.12), channel_id=1, source_target_pairs={{0,1},{1,2},{2,3},{3,4},{4,5},{5,6},{6,7},{7,8},{8,9},{9,10},{10,1... | collective-permute-start | bytes 192008 | tf_op jit(solution)/shard_map/ppermute | solution.py:15
  303.6 13.5 %slice-start = ((s8[7372800]{0:T(1024)(128)(4,1)}), s8[4194304]{0:T(1024)(128)(4,1)S(1)}, s32[]{:S(2)}) async-start(s8[7372800]{0:T(1024)(128)(4,1)} %bitcast.149), calls=%async_computation.2 | async-start | bytes 8388608
  305.6 9.6 %collective-permute-start.5 = (bf16[1,1,128,640]{3,2,1,0:T(8,128)(2,1)S(1)}, bf16[1,1,128,640]{3,2,1,0:T(8,128)(2,1)S(1)}, u32[]{:S(2)}, u32[]{:S(2)}) collective-permute-start(bf16[1,1,128,640]{3,2,1,0:T(8,128)(2,1)S(1)} %get-tuple-element.18), channel_id=1, source_target_pairs={{16,0},{32,16},{48,32},{64,48},{80,64},{96,80},{112,96},{17,1},{33... | collective-permute-start | bytes 491528 | tf_op jit(solution)/shard_map/ppermute | solution.py:18
  307.8 9.3 %slice-start.1 = ((s8[7372800]{0:T(1024)(128)(4,1)}), s8[3178496]{0:T(1024)(128)(4,1)S(1)}, s32[]{:S(2)}) async-start(s8[7372800]{0:T(1024)(128)(4,1)} %bitcast.149), calls=%async_computation.3 | async-start | bytes 6356992
  307.8 7.4 %collective-permute-start.4 = (bf16[1,1,128,640]{3,2,1,0:T(8,128)(2,1)S(1)}, bf16[1,1,128,640]{3,2,1,0:T(8,128)(2,1)S(1)}, u32[]{:S(2)}, u32[]{:S(2)}) collective-permute-start(bf16[1,1,128,640]{3,2,1,0:T(8,128)(2,1)S(1)} %get-tuple-element.17), channel_id=1, source_target_pairs={{0,16},{16,32},{32,48},{48,64},{64,80},{80,96},{96,112},{1,17},{17... | collective-permute-start | bytes 491528 | tf_op jit(solution)/shard_map/ppermute | solution.py:15
  338.3 3.8 copy-start.11
  354.3 45.2 %all-to-all-start.1 = ((bf16[1,12,128,640]{3,1,0,2:T(8,128)(2,1)}), bf16[1,12,128,640]{3,1,0,2:T(8,128)(2,1)S(1)}, u32[]{:S(2)}, u32[]{:S(2)}) async-start(bf16[1,12,128,640]{3,1,0,2:T(8,128)(2,1)} %copy.32), calls=%async_computation.1 | async-start | bytes 5242880 | tf_op jit(solution)/shard_map/all_to_all | solution.py:127
  362.6 5.7 %copy-start.4 = (bf16[50,33,640]{2,1,0:T(8,128)(2,1)S(1)}, bf16[50,33,640]{2,1,0:T(8,128)(2,1)}, u32[]{:S(2)}) copy-start(bf16[50,33,640]{2,1,0:T(8,128)(2,1)} %get-tuple-element.10) | copy-start | bytes 6336004
  368.3 5.2 %copy-start.2 = (bf16[50,33,640]{2,1,0:T(8,128)(2,1)S(1)}, bf16[50,33,640]{2,1,0:T(8,128)(2,1)}, u32[]{:S(2)}) copy-start(bf16[50,33,640]{2,1,0:T(8,128)(2,1)} %get-tuple-element.9) | copy-start | bytes 6336004
  403.0 5.4 %copy-start.3 = (bf16[50,33,640]{2,1,0:T(8,128)(2,1)S(1)}, bf16[50,33,640]{2,1,0:T(8,128)(2,1)}, u32[]{:S(2)}) copy-start(bf16[50,33,640]{2,1,0:T(8,128)(2,1)} %get-tuple-element.9) | copy-start | bytes 6336004
  403.0 5.4 %copy-start.10 = (f32[640]{0:T(1024)S(1)}, f32[640]{0:T(1024)}, u32[]{:S(2)}) copy-start(f32[640]{0:T(1024)} %param.15) | copy-start | bytes 7684
where the time goes:
time: 429 us; the launch traced here: 423 us
  blocking collectives  132 us (31%)
  local copies, waits for them, and re-layouts  121 us (28%)
  matrix products  93.1 us (22%)
  other arithmetic  34.7 us (8%)
  starting transfers between devices  29.9 us (7%)
  waiting for transfers between devices  11.4 us (3%)
    dot_general x18, matrix products, apply_taps(): jnp.einsum('...hwc,cd->...hwd', piece, kernel[tap_row, tap_col], preferre...  93.1 us
    psum x1, blocking collectives, per_device(): sum_local, sum_sub = lax.psum((sum_local, sum_sub), ('row', 'col'))  68.9 us
    psum x1, blocking collectives, per_device(): lax.psum((square_local, square_sub), ('row', 'col'))  62.9 us
    sub x2, local copies, waits for them, and re-layouts, activate(): subs - mean_sub[None, :, None, :, :, None]  34 us
    mul x2, local copies, waits for them, and re-layouts, activate(): (subs - mean_sub[None, :, None, :, :, None]) * lax.rsqrt(var_sub + 1e-05)...  33.9 us
    reshape x1, local copies, waits for them, and re-layouts, activate(): values.reshape(height // STRIDE, STRIDE, width // STRIDE, STRIDE, GROUPS,...  32 us
    all_to_all x1, waiting for transfers between devices, per_device(): lax.all_to_all(result, 'col', split_axis=2, concat_axis=0, tiled=True)  10.9 us
    ppermute x3, starting transfers between devices, extended(): lax.ppermute(lax.slice_in_dim(block, block.shape[dim] - width, None, axis...  10.5 us
  transfers between devices with their start and end apart: 8, of which 2 were waited for; matrix products, arithmetic and copies ran while one was open for 12% of the time, Pallas kernels for 0%

commit v1 on v0

v1 whole, which is shorter than its diff:
```python
import jax
import jax.numpy as jnp
from jax import lax
from jax.experimental import pallas as pl
from jax.experimental.pallas import tpu as pltpu
from jax.sharding import PartitionSpec as P

CH = 640
GROUPS = 32
PER_GROUP = 20
ROWS = 48
COLS = 32
PAIRS = ROWS // 2
KDIM = 3 * CH
F32 = jnp.float32
BF16 = jnp.bfloat16
MESH = pl.DeviceIdType.MESH
NROW = 8
NCOL = 16
LOCAL_COUNT = float((ROWS // 4) * (COLS // 4) * PER_GROUP)


def groups_to_lanes(part):
    chan = lax.broadcasted_iota(jnp.int32, (CH, 128), 0)
    lane = lax.broadcasted_iota(jnp.int32, (CH, 128), 1) - GROUPS * part
    first = lane * PER_GROUP
    return jnp.where((lane >= 0) & (chan >= first) & (chan < first + PER_GROUP), 1.0, 0.0).astype(F32)


def lanes_to_channels(part):
    lane = lax.broadcasted_iota(jnp.int32, (128, CH), 0) - GROUPS * part
    chan = lax.broadcasted_iota(jnp.int32, (128, CH), 1)
    first = lane * PER_GROUP
    return jnp.where((lane >= 0) & (chan >= first) & (chan < first + PER_GROUP), 1.0, 0.0).astype(F32)


def exact_dot(a, b):
    return lax.dot_general(
        a, b, (((1,), (0,)), ((), ())), precision=lax.Precision.HIGHEST, preferred_element_type=F32
    )


def fold_half(tile):
    return tile + pltpu.roll(tile, 4, 0)


def merge(tiles, count):
    number = len(tiles)
    average = tiles[0]
    for tile in tiles[1:]:
        average = average + tile
    total = average
    average = average * (1.0 / number)
    spread = None
    for tile in tiles:
        gap = tile - average
        spread = gap * gap if spread is None else spread + gap * gap
    rows = lax.broadcasted_iota(jnp.int32, (8, 128), 0)
    return jnp.where(rows < 4, average, total + count * pltpu.roll(spread, 4, 0))


def gather_kernel(
    lat_hbm, kl_hbm, kd_hbm, blend_ref,
    lat, top, bot, left, right, stats, wl, wd, wgt,
    mid_l, mid_d, strip_l, strip_r, tile1, tile2, got1, got2,
    sem_in, sem_w, send_h, recv_h, send1, recv1, send2, recv2,
):
    row = lax.axis_index("row")
    col = lax.axis_index("col")
    has_up = row > 0
    has_dn = row < NROW - 1
    has_lf = col > 0
    has_rt = col < NCOL - 1

    load = pltpu.make_async_copy(lat_hbm, lat, sem_in)
    load.start()
    weights = []
    for n, (src, planes, mid) in enumerate(((kd_hbm, wd, mid_d), (kl_hbm, wl, mid_l))):
        for m, (a, dst) in enumerate(((0, planes.at[0]), (1, mid), (2, planes.at[3]))):
            copy = pltpu.make_async_copy(src.at[a], dst, sem_w.at[3 * n + m])
            copy.start()
            weights.append(copy)

    barrier = pltpu.get_barrier_semaphore()
    for d in range(1, NROW):
        pl.semaphore_signal(barrier, 1, device_id=(lax.rem(row + d, NROW), col), device_id_type=MESH)
    for d in range(1, NCOL):
        pl.semaphore_signal(barrier, 1, device_id=(row, lax.rem(col + d, NCOL)), device_id_type=MESH)
    for dr, okr in ((-1, has_up), (1, has_dn)):
        for dc, okc in ((-1, has_lf), (1, has_rt)):
            @pl.when(okr & okc)
            def _():
                pl.semaphore_signal(barrier, 1, device_id=(row + dr, col + dc), device_id_type=MESH)

    load.wait()

    @pl.loop(0, ROWS // 4)
    def _(k):
        for strip, start, part in ((strip_l, 0, 0), (strip_r, 16, 12)):
            pieces = [
                lat[4 * k + p, pl.ds(start, 16), :].astype(F32)[part : part + 4] for p in range(4)
            ]
            strip[k] = jnp.concatenate(pieces, axis=0).astype(BF16)

    diagonals = (jnp.where(has_up, 1, 0) + jnp.where(has_dn, 1, 0)) * (
        jnp.where(has_lf, 1, 0) + jnp.where(has_rt, 1, 0)
    )
    pl.semaphore_wait(barrier, NROW - 1 + NCOL - 1 + diagonals)

    last = ROWS // 4 - 1
    halos = []
    for n, (src, dst, dr, dc, ok, got) in enumerate((
        (lat.at[pl.ds(ROWS - 4, 4)], top, 1, 0, has_dn, has_up),
        (lat.at[pl.ds(0, 4)], bot, -1, 0, has_up, has_dn),
        (strip_r, left.at[pl.ds(1, ROWS // 4)], 0, 1, has_rt, has_lf),
        (strip_l, right.at[pl.ds(1, ROWS // 4)], 0, -1, has_lf, has_rt),
        (strip_r.at[last], left.at[0], 1, 1, has_dn & has_rt, has_up & has_lf),
        (strip_r.at[0], left.at[ROWS // 4 + 1], -1, 1, has_up & has_rt, has_dn & has_lf),
        (strip_l.at[last], right.at[0], 1, -1, has_dn & has_lf, has_up & has_rt),
        (strip_l.at[0], right.at[ROWS // 4 + 1], -1, -1, has_up & has_lf, has_dn & has_rt),
    )):
        copy = pltpu.make_async_remote_copy(
            src_ref=src, dst_ref=dst, send_sem=send_h.at[n], recv_sem=recv_h.at[n],
            device_id=(row + dr, col + dc), device_id_type=MESH,
        )
        halos.append((copy, ok, got))

    def sums(k, acc):
        out = []
        for p in range(4):
            x = lat[4 * k + p].astype(F32)
            out.append(acc[p] + ((x[0:8] + x[8:16]) + (x[16:24] + x[24:32])))
        return tuple(out)

    zero = tuple(jnp.zeros((8, CH), F32) for _ in range(4))
    acc = lax.fori_loop(0, ROWS // 4, sums, zero)
    mean = None
    for p in range(4):
        term = exact_dot(acc[p], groups_to_lanes(p))
        mean = term if mean is None else mean + term
    mean = fold_half(mean) * (1.0 / LOCAL_COUNT)
    centre = [exact_dot(mean, lanes_to_channels(p)) for p in range(4)]

    def squares(k, acc):
        out = []
        for p in range(4):
            x = lat[4 * k + p].astype(F32)
            term = None
            for s in range(4):
                gap = x[8 * s : 8 * s + 8] - centre[p]
                term = gap * gap if term is None else term + gap * gap
            out.append(acc[p] + term)
        return tuple(out)

    acc = lax.fori_loop(0, ROWS // 4, squares, zero)
    square = None
    for p in range(4):
        term = exact_dot(acc[p], groups_to_lanes(p))
        square = term if square is None else square + term
    square = fold_half(square)
    rows8 = lax.broadcasted_iota(jnp.int32, (8, 128), 0)
    tile1[...] = jnp.where(rows8 < 4, mean, square)

    first = []
    for d in range(1, NROW):
        copy = pltpu.make_async_remote_copy(
            src_ref=tile1, dst_ref=got1.at[d], send_sem=send1.at[d], recv_sem=recv1.at[d],
            device_id=(lax.rem(row + d, NROW), col), device_id_type=MESH,
        )
        copy.start()
        first.append(copy)

    for copy, ok, _ in halos:
        @pl.when(ok)
        def _():
            copy.start()

    def planes(dst, mid):
        @pl.loop(0, KDIM // 32)
        def _(i):
            at = pl.ds(pl.multiple_of(i * 32, 32), 32)
            ends = dst[0, at, :].astype(F32) + dst[3, at, :].astype(F32)
            centre_tap = mid[at, :].astype(F32)
            dst[1, at, :] = ((ends + centre_tap) * 0.5).astype(BF16)
            dst[2, at, :] = ((ends - centre_tap) * 0.5).astype(BF16)

    share = blend_ref[...].astype(F32) * 0.25
    turned = share.T
    for r in range(ROWS):
        wgt[pl.ds(r * COLS, COLS), :] = jnp.broadcast_to(turned[:, r : r + 1], (COLS, 128))

    for copy in first:
        copy.wait_recv()
    tile2[...] = merge([tile1[...]] + [got1[d] for d in range(1, NROW)], LOCAL_COUNT)
    second = []
    for d in range(1, NCOL):
        copy = pltpu.make_async_remote_copy(
            src_ref=tile2, dst_ref=got2.at[d], send_sem=send2.at[d], recv_sem=recv2.at[d],
            device_id=(row, lax.rem(col + d, NCOL)), device_id_type=MESH,
        )
        copy.start()
        second.append(copy)

    for copy in weights[:3]:
        copy.wait()
    planes(wd, mid_d)
    for copy in weights[3:]:
        copy.wait()
    planes(wl, mid_l)

    for copy in second:
        copy.wait_recv()
    count = LOCAL_COUNT * NROW
    tile = merge([tile2[...]] + [got2[d] for d in range(1, NCOL)], count)
    count = count * NCOL
    mean = jnp.where(rows8 < 4, tile, pltpu.roll(tile, 4, 0))
    square = jnp.where(rows8 < 4, pltpu.roll(tile, 4, 0), tile)

    def everywhere(v):
        for step in (1, 2, 4):
            v = v + pltpu.roll(v, step, 0)
        for step in (32, 64):
            v = v + pltpu.roll(v, step, 1)
        return v * (1.0 / 32.0)

    mean_all = everywhere(mean)
    gap = mean - mean_all
    var_all = everywhere(square * (1.0 / count) + gap * gap)
    var = square * (1.0 / count)
    stats[pl.ds(0, 8)] = mean
    stats[pl.ds(8, 8)] = lax.rsqrt(var + 1e-05)
    stats[pl.ds(16, 8)] = mean_all
    stats[pl.ds(24, 8)] = lax.rsqrt(var_all + 1e-05)

    for copy, ok, got in halos:
        @pl.when(got)
        def _():
            copy.wait_recv()

        @pl.when(ok)
        def _():
            copy.wait_send()
    for copy in first + second:
        copy.wait_send()


def conv_kernel(
    lat, top, bot, left, right, stats, wl, wd, wgt,
    gam_l, bet_l, bia_l, gam_d, bet_d, bia_d,
    out,
    act_l, act_d, lhs, sum_l, sum_d, scale_d, shift_d, scale_e, shift_e,
):
    row = lax.axis_index("row")
    col = lax.axis_index("col")
    has_up = row > 0
    has_dn = row < NROW - 1
    has_lf = col > 0
    has_rt = col < NCOL - 1

    half = 0.5
    for p in range(4):
        spread = exact_dot(stats[pl.ds(0, 16)], lanes_to_channels(p))
        scale = spread[8:16] * (gam_d[...] * half)
        shift = bet_d[...] * half - spread[0:8] * scale
        scale_d[p] = scale
        shift_d[p] = shift
        scale_e[pl.ds(4 * p, 4)] = scale[0:4]
        shift_e[pl.ds(4 * p, 4)] = shift[0:4]
    spread = exact_dot(stats[pl.ds(16, 16)], lanes_to_channels(0))
    scale_l = spread[8:16] * (gam_l[...] * half)
    shift_l = bet_l[...] * half - spread[0:8] * scale_l

    def silu(x, scale, shift):
        h = x * scale + shift
        return h + h * jnp.tanh(h)

    def put_row(dst, r, src, i, p):
        for ct in range(5):
            lanes = pl.ds(ct * 128, 128)
            x = src[i, :, lanes].astype(F32)
            cut = slice(ct * 128, ct * 128 + 128)
            sd, td = scale_d[p, :, lanes], shift_d[p, :, lanes]
            sl, tl = scale_l[:, cut], shift_l[:, cut]
            for s in range(4):
                piece = x[8 * s : 8 * s + 8]
                act_d[ct, r, pl.ds(8 + 8 * s, 8), :] = silu(piece, sd, td)
                act_l[ct, r, pl.ds(8 + 8 * s, 8), :] = silu(piece, sl, tl)

    @pl.loop(0, ROWS // 4)
    def _(k):
        for p in range(4):
            put_row(None, 4 * k + p + 4, lat, 4 * k + p, p)

    for src, base, ok in ((top, 0, has_up), (bot, ROWS + 4, has_dn)):
        @pl.when(ok)
        def _():
            for p in range(4):
                put_row(None, base + p, src, p, p)

        @pl.when(jnp.logical_not(ok))
        def _():
            for p in range(4):
                for ct in range(5):
                    act_d[ct, base + p] = jnp.zeros((48, 128), F32)
                    act_l[ct, base + p] = jnp.zeros((48, 128), F32)

    for src, at, ok in ((left, 4, has_lf), (right, 40, has_rt)):
        for k0, k1, okr in ((0, 1, has_up), (1, 13, None), (13, 14, has_dn)):
            good = ok if okr is None else ok & okr

            @pl.when(good)
            def _():
                @pl.loop(k0, k1)
                def _(k):
                    for ct in range(5):
                        lanes = pl.ds(ct * 128, 128)
                        cut = slice(ct * 128, ct * 128 + 128)
                        x = src[k, :, lanes].astype(F32)
                        vd = silu(x, scale_e[:, lanes], shift_e[:, lanes])
                        vl = silu(x, scale_l[0:1, cut], shift_l[0:1, cut])
                        for p in range(4):
                            act_d[ct, 4 * k + p, pl.ds(at, 4), :] = vd[4 * p : 4 * p + 4]
                            act_l[ct, 4 * k + p, pl.ds(at, 4), :] = vl[4 * p : 4 * p + 4]

            @pl.when(jnp.logical_not(good))
            def _():
                @pl.loop(k0, k1)
                def _(k):
                    for ct in range(5):
                        for p in range(4):
                            act_d[ct, 4 * k + p, pl.ds(at, 4), :] = jnp.zeros((4, 128), F32)
                            act_l[ct, 4 * k + p, pl.ds(at, 4), :] = jnp.zeros((4, 128), F32)

    mixes = ((0, 2, -1), (1, 2, 1), (2, 1, -1), (1, 3, -1))
    for act, planes, total, bias, near, shifts in (
        (act_d, wd, sum_d, bia_d, 4, (4, 8, 12)),
        (act_l, wl, sum_l, bia_l, 1, (7, 8, 9)),
    ):
        for k in range(4):
            i, j, sign = mixes[k]

            @pl.loop(0, PAIRS)
            def _(t):
                if near == 4:
                    base = 8 * (t // 4) + t % 4
                else:
                    base = 2 * t + 3
                at = pl.ds(pl.multiple_of(t * COLS, COLS), COLS)
                for b in range(3):
                    for ct in range(5):
                        one = act[ct, base + near * i, pl.ds(shifts[b], COLS), :]
                        two = act[ct, base + near * j, pl.ds(shifts[b], COLS), :]
                        mixed = one + two if sign > 0 else one - two
                        lhs[at, pl.ds(b * CH + ct * 128, 128)] = mixed.astype(BF16)

            for n, width in ((0, 256), (256, 256), (512, 128)):
                at = pl.ds(n, width)
                m = jnp.dot(lhs[...], planes[k, :, at], preferred_element_type=F32)
                if k == 0:
                    total[0, :, at] = m + bias[:, at]
                elif k == 1:
                    total[0, :, at] += m
                    total[1, :, at] = m + bias[:, at]
                elif k == 2:
                    total[0, :, at] += m
                    total[1, :, at] -= m
                else:
                    total[1, :, at] -= m

    @pl.loop(0, ROWS // 8)
    def _(u):
        for h in range(2):
            for p in range(4):
                r = 8 * u + 4 * h + p
                from_d = pl.ds(pl.multiple_of((4 * u + p) * COLS, COLS), COLS)
                from_l = pl.ds(pl.multiple_of((4 * u + 2 * h + p // 2) * COLS, COLS), COLS)
                w = wgt[pl.ds(pl.multiple_of(r * COLS, COLS), COLS), :]
                for ct in range(5):
                    lanes = pl.ds(ct * 128, 128)
                    dil = sum_d[h, from_d, lanes].astype(BF16).astype(F32)
                    loc = sum_l[p % 2, from_l, lanes]
                    out[r, :, lanes] = (w * loc + (1.0 - w) * dil).astype(BF16)


VM = pl.BlockSpec(memory_space=pltpu.VMEM)
ANY = pl.BlockSpec(memory_space=pl.ANY)


def per_device(
    latent, blend, gamma_local, beta_local, kernel_local, bias_local,
    gamma_dilated, beta_dilated, kernel_dilated, bias_dilated,
):
    kl = kernel_local.reshape(3, KDIM, CH)
    kd = kernel_dilated.reshape(3, KDIM, CH)
    dma = pltpu.SemaphoreType.DMA
    gathered = pl.pallas_call(
        gather_kernel,
        out_shape=(
            pltpu.VMEM((ROWS, COLS, CH), BF16),
            pltpu.VMEM((4, COLS, CH), BF16),
            pltpu.VMEM((4, COLS, CH), BF16),
            pltpu.VMEM((ROWS // 4 + 2, 16, CH), BF16),
            pltpu.VMEM((ROWS // 4 + 2, 16, CH), BF16),
            pltpu.VMEM((32, 128), F32),
            pltpu.VMEM((4, KDIM, CH), BF16),
            pltpu.VMEM((4, KDIM, CH), BF16),
            pltpu.VMEM((ROWS * COLS, 128), F32),
        ),
        in_specs=[ANY, ANY, ANY, VM],
        out_specs=(VM,) * 9,
        scratch_shapes=[
            pltpu.VMEM((KDIM, CH), BF16),
            pltpu.VMEM((KDIM, CH), BF16),
            pltpu.VMEM((ROWS // 4, 16, CH), BF16),
            pltpu.VMEM((ROWS // 4, 16, CH), BF16),
            pltpu.VMEM((8, 128), F32),
            pltpu.VMEM((8, 128), F32),
            pltpu.VMEM((NROW, 8, 128), F32),
            pltpu.VMEM((NCOL, 8, 128), F32),
            dma, dma((6,)), dma((8,)), dma((8,)),
            dma((NROW,)), dma((NROW,)), dma((NCOL,)), dma((NCOL,)),
        ],
        compiler_params=pltpu.CompilerParams(
            collective_id=0, has_side_effects=True, vmem_limit_bytes=10 * 2**20
        ),
        name="gather",
    )(latent, kl, kd, blend)
    gathered = [pltpu.with_memory_space_constraint(a, pltpu.VMEM) for a in gathered]
    small = [
        a.reshape(1, CH)
        for a in (gamma_local, beta_local, bias_local, gamma_dilated, beta_dilated, bias_dilated)
    ]
    return pl.pallas_call(
        conv_kernel,
        out_shape=jax.ShapeDtypeStruct((ROWS, COLS, CH), BF16),
        in_specs=[VM] * 15,
        out_specs=VM,
        scratch_shapes=[
            pltpu.VMEM((5, 56, 48, 128), F32),
            pltpu.VMEM((5, 56, 48, 128), F32),
            pltpu.VMEM((PAIRS * COLS, KDIM), BF16),
            pltpu.VMEM((2, PAIRS * COLS, CH), F32),
            pltpu.VMEM((2, PAIRS * COLS, CH), F32),
            pltpu.VMEM((4, 8, CH), F32),
            pltpu.VMEM((4, 8, CH), F32),
            pltpu.VMEM((16, CH), F32),
            pltpu.VMEM((16, CH), F32),
        ],
        compiler_params=pltpu.CompilerParams(vmem_limit_bytes=32 * 2**20),
        name="conv",
    )(*gathered, *small)


def solution(mesh):
    placed = (P("row", "col", None), P("row", "col"), P(), P(), P(), P(), P(), P(), P(), P())
    return jax.shard_map(
        per_device, mesh=mesh, in_specs=placed, out_specs=P("row", "col", None), check_vma=False
    )
```

time: 429 us -> 79 us (0.18); the launches traced: 423 us -> 78.5 us
  blocking collectives: 132 us -> 0 us
  local copies, waits for them, and re-layouts: 121 us -> 16.2 us
  matrix products: 93.1 us -> 0 us
  Pallas kernels: 0 us -> 62.3 us
  other arithmetic: 34.7 us -> 0 us
  starting transfers between devices: 29.9 us -> 0 us
  waiting for transfers between devices: 11.4 us -> 0 us
    psum x2 -> x0, blocking collectives: 132 us -> none  [the longest x1 68.9 us: per_device(): sum_local, sum_sub = lax.psum((sum_local, sum_sub), ('row', 'col'))]
    dot_general x18 -> x0, matrix products: 93.1 us -> none  [apply_taps(): jnp.einsum('...hwc,cd->...hwd', piece, kernel[tap_row, tap_col], preferre...]
    pallas_call x0 -> x2, Pallas kernels: none -> 62.3 us  [the longest x1 38.2 us: per_device(): pl.pallas_call(conv_kernel, out_shape=jax.ShapeDtypeStruct((ROWS, COLS, C...]
    sub x5 -> x0, local copies, waits for them, and re-layouts: 34.2 us -> none  [the longest x2 34 us: activate(): subs - mean_sub[None, :, None, :, :, None]]
    mul x4 -> x0, local copies, waits for them, and re-layouts: 34.1 us -> none  [the longest x2 33.9 us: activate(): (subs - mean_sub[None, :, None, :, :, None]) * lax.rsqrt(var_sub + 1e-05)...]
    reshape x3 -> x6, local copies, waits for them, and re-layouts: 39.6 us -> 7.65 us  [per_device(): a.reshape(1, CH)]
    reduce_sum x6 -> x0, other arithmetic: 21.4 us -> none  [the longest x1 10.4 us: per_device(): square_sub = jnp.sum(centered_sub * centered_sub, axis=(0, 2, 5))]
    ppermute x6 -> x0, starting transfers between devices: 16.8 us -> none  [the longest x3 10.5 us: extended(): lax.ppermute(lax.slice_in_dim(block, block.shape[dim] - width, None, axis...]
  transfers between devices with their start and end apart: 8 -> 0, of which waited for: 2 -> 0; matrix products, arithmetic and copies ran while one was open for 12% -> 0% of each run, Pallas kernels for 0% -> 0%
where the time goes in v1:
time: 79 us; the launch traced here: 78.5 us
  Pallas kernels  62.3 us (79%)
  local copies, waits for them, and re-layouts  16.2 us (21%)
    pallas_call x1, Pallas kernels, per_device(): pl.pallas_call(conv_kernel, out_shape=jax.ShapeDtypeStruct((ROWS, COLS, C...  38.2 us
    pallas_call x1, Pallas kernels, per_device(): pl.pallas_call(gather_kernel, out_shape=(pltpu.VMEM((ROWS, COLS, CH), BF1...  24.1 us
    unnamed x7, local copies, waits for them, and re-layouts  8.52 us
    reshape x6, local copies, waits for them, and re-layouts, per_device(): a.reshape(1, CH)  7.65 us

profile of v1, /device:TPU:1, one launch (start us, length us, event | category | flops | bytes accessed | tf_op | source)
XLA Modules:
  0.0 78.5 jit_solution(7904687441427014444)
XLA Ops:
  0.0 1.3 %reshape.26.gam_l = f32[1,640]{1,0:T(1,128)} reshape(f32[640]{0:T(1024)} %param.12) | data formatting | bytes 5120 | tf_op jit(solution)/shard_map/reshape | solution.py:430
  1.3 1.3 %reshape.27.bet_l = f32[1,640]{1,0:T(1,128)} reshape(f32[640]{0:T(1024)} %param.13) | data formatting | bytes 5120 | tf_op jit(solution)/shard_map/reshape | solution.py:430
  2.5 1.3 %reshape.28.bia_l = f32[1,640]{1,0:T(1,128)} reshape(f32[640]{0:T(1024)} %param.15) | data formatting | bytes 5120 | tf_op jit(solution)/shard_map/reshape | solution.py:430
  3.8 1.3 %reshape.29.gam_d = f32[1,640]{1,0:T(1,128)} reshape(f32[640]{0:T(1024)} %param.16) | data formatting | bytes 5120 | tf_op jit(solution)/shard_map/reshape | solution.py:430
  5.1 1.3 %reshape.30.bet_d = f32[1,640]{1,0:T(1,128)} reshape(f32[640]{0:T(1024)} %param.17) | data formatting | bytes 5120 | tf_op jit(solution)/shard_map/reshape | solution.py:430
  6.4 1.3 %reshape.31.bia_d = f32[1,640]{1,0:T(1,128)} reshape(f32[640]{0:T(1024)} %param.19) | data formatting | bytes 5120 | tf_op jit(solution)/shard_map/reshape | solution.py:430
  7.7 0.8 %copy.11.blend_ref = s32[48,32]{1,0:T(8,128)S(1)} copy(s32[48,32]{0,1:T(8,128)} %param.11) | data formatting | bytes 12288 | tf_op args[1]
  8.4 0.0 copy-start
  8.4 3.1 %copy-done = bf16[3,3,640,640]{3,2,1,0:T(8,128)(2,1)S(1)} copy-done((bf16[3,3,640,640]{3,2,1,0:T(8,128)(2,1)S(1)}, bf16[3,3,640,640]{3,2,1,0:T(8,128)(2,1)}, u32[]{:S(2)}) %copy-start) | copy-done | bytes 7372824
  11.5 0.0 copy-start.1
  11.5 3.1 %copy-done.1 = bf16[3,3,640,640]{3,2,1,0:T(8,128)(2,1)S(1)} copy-done((bf16[3,3,640,640]{3,2,1,0:T(8,128)(2,1)S(1)}, bf16[3,3,640,640]{3,2,1,0:T(8,128)(2,1)}, u32[]{:S(2)}) %copy-start.1) | copy-done | bytes 7372824
  14.6 0.0 copy-start.2
  14.6 1.5 %copy-done.2 = bf16[48,32,640]{2,1,0:T(8,128)(2,1)S(1)} copy-done((bf16[48,32,640]{2,1,0:T(8,128)(2,1)S(1)}, bf16[48,32,640]{2,1,0:T(8,128)(2,1)}, u32[]{:S(2)}) %copy-start.2) | copy-done | bytes 1966104
  16.2 24.1 %gather.1 = (bf16[48,32,640]{2,1,0:T(8,128)(2,1)S(1)}, bf16[4,32,640]{2,1,0:T(8,128)(2,1)S(1)}, bf16[4,32,640]{2,1,0:T(8,128)(2,1)S(1)}, bf16[14,16,640]{2,1,0:T...) custom-call(bf16[48,32,640]{2,1,0:T(8,128)(2,1)S(1)} %copy-done.2, ...), custom_call_target="tpu_custom_call" | custom-call | tf_op jit(solution)/shard_map/gather/pallas_call | solution.py:396
  40.2 38.2 %conv.1 = bf16[48,32,640]{2,1,0:T(8,128)(2,1)} custom-call(bf16[48,32,640]{2,1,0:T(8,128)(2,1)S(1)} %get-tuple-element.14.lat, bf16[4,32,640]{2,1,0:T(8,128)(2,1)S(1)} %get-tuple-element.15.top, bf16[4,32,640]{2,1,0:T(8,128)(2,1)S(1)} %get-tuple-element.16.bot, bf16[14,16,640]{2,1,0:T(8,128)(2,1)S(1)} %get-tuple-element.17.left, ...), custom_call_target="tpu_custom_call" | custom-call | tf_op jit(solution)/shard_map/conv/pallas_call | solution.py:433
Async XLA Ops:
  8.4 3.1 %copy-start = (bf16[3,3,640,640]{3,2,1,0:T(8,128)(2,1)S(1)}, bf16[3,3,640,640]{3,2,1,0:T(8,128)(2,1)}, u32[]{:S(2)}) copy-start(bf16[3,3,640,640]{3,2,1,0:T(8,128)(2,1)} %param.14) | copy-start | bytes 22118404
  11.5 3.1 %copy-start.1 = (bf16[3,3,640,640]{3,2,1,0:T(8,128)(2,1)S(1)}, bf16[3,3,640,640]{3,2,1,0:T(8,128)(2,1)}, u32[]{:S(2)}) copy-start(bf16[3,3,640,640]{3,2,1,0:T(8,128)(2,1)} %param.18) | copy-start | bytes 22118404
  14.6 1.5 %copy-start.2 = (bf16[48,32,640]{2,1,0:T(8,128)(2,1)S(1)}, bf16[48,32,640]{2,1,0:T(8,128)(2,1)}, u32[]{:S(2)}) copy-start(bf16[48,32,640]{2,1,0:T(8,128)(2,1)} %lat_hbm.1) | copy-start | bytes 5898244

commit v2 on v1

v2 whole, which is shorter than its diff:
```python
import jax
import jax.numpy as jnp
from jax import lax
from jax.experimental import pallas as pl
from jax.experimental.pallas import tpu as pltpu
from jax.sharding import PartitionSpec as P

CH = 640
GROUPS = 32
PER_GROUP = 20
ROWS = 48
COLS = 32
PAIRS = ROWS // 2
KDIM = 3 * CH
F32 = jnp.float32
BF16 = jnp.bfloat16
MESH = pl.DeviceIdType.MESH
NROW = 8
NCOL = 16
UNITS = ROWS // 4
STEPS = COLS // 4
LOCAL_COUNT = float(UNITS * STEPS * PER_GROUP)


def groups_to_lanes(first_lane):
    chan = lax.broadcasted_iota(jnp.int32, (CH, 128), 0)
    lane = lax.broadcasted_iota(jnp.int32, (CH, 128), 1) - first_lane
    first = lane * PER_GROUP
    inside = (lane >= 0) & (chan >= first) & (chan < first + PER_GROUP)
    return jnp.where(inside, 1.0, 0.0).astype(F32)


def lanes_to_channels():
    lane = lax.broadcasted_iota(jnp.int32, (128, CH), 0)
    chan = lax.broadcasted_iota(jnp.int32, (128, CH), 1)
    first = lane * PER_GROUP
    return jnp.where((chan >= first) & (chan < first + PER_GROUP), 1.0, 0.0).astype(F32)


def exact_dot(a, b):
    return lax.dot_general(
        a, b, (((1,), (0,)), ((), ())), precision=lax.Precision.HIGHEST, preferred_element_type=F32
    )


def merge(tiles, count):
    number = len(tiles)
    total = tiles[0]
    for tile in tiles[1:]:
        total = total + tile
    average = total * (1.0 / number)
    spread = None
    for tile in tiles:
        gap = tile - average
        spread = gap * gap if spread is None else spread + gap * gap
    lanes = lax.broadcasted_iota(jnp.int32, (16, 128), 1)
    return jnp.where(lanes < GROUPS, average, total + count * pltpu.roll(spread, GROUPS, 1))


def gather_kernel(
    lat_hbm, kl_hbm, kd_hbm, blend_hbm,
    xd, xn, stats, wl, wd, wgt,
    lat, blend_ref, mid_l, mid_d, tile1, tile2, got1, got2,
    sem_in, sem_b, sem_w, send_h, recv_h, send1, recv1, send2, recv2,
):
    row = lax.axis_index("row")
    col = lax.axis_index("col")
    has_up = row > 0
    has_dn = row < NROW - 1
    has_lf = col > 0
    has_rt = col < NCOL - 1

    load = pltpu.make_async_copy(lat_hbm, lat, sem_in)
    load.start()
    load_blend = pltpu.make_async_copy(blend_hbm, blend_ref, sem_b)
    load_blend.start()
    weights = []
    for n, (src, planes, mid) in enumerate(((kd_hbm, wd, mid_d), (kl_hbm, wl, mid_l))):
        for m, (a, dst) in enumerate(((0, planes.at[0]), (1, mid), (2, planes.at[3]))):
            copy = pltpu.make_async_copy(src.at[a], dst, sem_w.at[3 * n + m])
            copy.start()
            weights.append(copy)

    barrier = pltpu.get_barrier_semaphore()
    for d in range(1, NROW):
        pl.semaphore_signal(barrier, 1, device_id=(lax.rem(row + d, NROW), col), device_id_type=MESH)
    for d in range(1, NCOL):
        pl.semaphore_signal(barrier, 1, device_id=(row, lax.rem(col + d, NCOL)), device_id_type=MESH)
    for dr, okr in ((-1, has_up), (1, has_dn)):
        for dc, okc in ((-1, has_lf), (1, has_rt)):
            @pl.when(okr & okc)
            def _():
                pl.semaphore_signal(barrier, 1, device_id=(row + dr, col + dc), device_id_type=MESH)

    load.wait()

    def arrange(u, acc):
        rows = []
        for p in range(4):
            x = lat[4 * u + p].astype(F32)
            for ct in range(5):
                xn[ct, 4 * u + p + 1, pl.ds(8, COLS), :] = x[:, ct * 128 : ct * 128 + 128]
            rows.append(x)
        for j in range(STEPS):
            cells = jnp.concatenate([x[4 * j : 4 * j + 4] for x in rows], axis=0)
            acc = acc + cells
            xd[u + 1, j + 1] = cells.astype(BF16)
        return acc

    acc = lax.fori_loop(0, UNITS, arrange, jnp.zeros((16, CH), F32))
    mean = exact_dot(acc, groups_to_lanes(0)) * (1.0 / LOCAL_COUNT)
    centre = exact_dot(mean, lanes_to_channels())

    def squares(u, acc):
        for j in range(STEPS):
            gap = xd[u + 1, j + 1].astype(F32) - centre
            acc = acc + gap * gap
        return acc

    acc = lax.fori_loop(0, UNITS, squares, jnp.zeros((16, CH), F32))
    square = exact_dot(acc, groups_to_lanes(GROUPS))
    lanes = lax.broadcasted_iota(jnp.int32, (16, 128), 1)
    tile1[...] = jnp.where(lanes < GROUPS, mean, square)

    diagonals = (jnp.where(has_up, 1, 0) + jnp.where(has_dn, 1, 0)) * (
        jnp.where(has_lf, 1, 0) + jnp.where(has_rt, 1, 0)
    )
    pl.semaphore_wait(barrier, NROW - 1 + NCOL - 1 + diagonals)

    first = []
    for d in range(1, NROW):
        copy = pltpu.make_async_remote_copy(
            src_ref=tile1, dst_ref=got1.at[d], send_sem=send1.at[d], recv_sem=recv1.at[d],
            device_id=(lax.rem(row + d, NROW), col), device_id_type=MESH,
        )
        copy.start()
        first.append(copy)

    halos = []
    inner_u, inner_j = pl.ds(1, UNITS), pl.ds(1, STEPS)
    for n, (src, dst, dr, dc, ok, got) in enumerate((
        (xd.at[inner_u, STEPS], xd.at[inner_u, 0], 0, 1, has_rt, has_lf),
        (xd.at[inner_u, 1], xd.at[inner_u, STEPS + 1], 0, -1, has_lf, has_rt),
        (xd.at[UNITS, inner_j], xd.at[0, inner_j], 1, 0, has_dn, has_up),
        (xd.at[1, inner_j], xd.at[UNITS + 1, inner_j], -1, 0, has_up, has_dn),
        (xd.at[UNITS, STEPS], xd.at[0, 0], 1, 1, has_dn & has_rt, has_up & has_lf),
        (xd.at[1, STEPS], xd.at[UNITS + 1, 0], -1, 1, has_up & has_rt, has_dn & has_lf),
        (xd.at[UNITS, 1], xd.at[0, STEPS + 1], 1, -1, has_dn & has_lf, has_up & has_rt),
        (xd.at[1, 1], xd.at[UNITS + 1, STEPS + 1], -1, -1, has_up & has_lf, has_dn & has_rt),
    )):
        copy = pltpu.make_async_remote_copy(
            src_ref=src, dst_ref=dst, send_sem=send_h.at[n], recv_sem=recv_h.at[n],
            device_id=(row + dr, col + dc), device_id_type=MESH,
        )
        halos.append((copy, ok, got))
        @pl.when(ok)
        def _():
            copy.start()

    def planes(dst, mid):
        @pl.loop(0, KDIM // 32)
        def _(i):
            at = pl.ds(pl.multiple_of(i * 32, 32), 32)
            ends = dst[0, at, :].astype(F32) + dst[3, at, :].astype(F32)
            centre_tap = mid[at, :].astype(F32)
            dst[1, at, :] = ((ends + centre_tap) * 0.5).astype(BF16)
            dst[2, at, :] = ((ends - centre_tap) * 0.5).astype(BF16)

    load_blend.wait()
    turned = blend_ref[...].astype(F32) * 0.25
    for r in range(ROWS):
        wgt[pl.ds(r * COLS, COLS), :] = jnp.broadcast_to(turned[:, r : r + 1], (COLS, 128))

    for copy in first:
        copy.wait_recv()
    tile2[...] = merge([tile1[...]] + [got1[d] for d in range(1, NROW)], LOCAL_COUNT)
    second = []
    for d in range(1, NCOL):
        copy = pltpu.make_async_remote_copy(
            src_ref=tile2, dst_ref=got2.at[d], send_sem=send2.at[d], recv_sem=recv2.at[d],
            device_id=(row, lax.rem(col + d, NCOL)), device_id_type=MESH,
        )
        copy.start()
        second.append(copy)

    for copy in weights[:3]:
        copy.wait()
    planes(wd, mid_d)
    for copy in weights[3:]:
        copy.wait()
    planes(wl, mid_l)

    for copy, ok, got in halos:
        @pl.when(got)
        def _():
            copy.wait_recv()

        @pl.when(ok)
        def _():
            copy.wait_send()

    for src, at in ((0, 0), (UNITS + 1, ROWS + 1)):
        part = 12 if src == 0 else 0
        for j in range(STEPS):
            x = xd[src, j + 1].astype(F32)[part : part + 4]
            for ct in range(5):
                xn[ct, at, pl.ds(8 + 4 * j, 4), :] = x[:, ct * 128 : ct * 128 + 128]
    for j, q, at in ((0, 3, 7), (STEPS + 1, 0, 8 + COLS)):
        @pl.loop(0, UNITS)
        def _(u):
            x = xd[u + 1, j].astype(F32)
            for p in range(4):
                for ct in range(5):
                    cell = x[4 * p + q : 4 * p + q + 1, ct * 128 : ct * 128 + 128]
                    xn[ct, 4 * u + p + 1, pl.ds(at, 1), :] = cell
        for src, p, r in ((0, 3, 0), (UNITS + 1, 0, ROWS + 1)):
            x = xd[src, j].astype(F32)
            for ct in range(5):
                cell = x[4 * p + q : 4 * p + q + 1, ct * 128 : ct * 128 + 128]
                xn[ct, r, pl.ds(at, 1), :] = cell

    for copy in second:
        copy.wait_recv()
    count = LOCAL_COUNT * NROW
    tile = merge([tile2[...]] + [got2[d] for d in range(1, NCOL)], count)
    count = count * NCOL
    square = pltpu.roll(tile, 128 - GROUPS, 1)

    def everywhere(v):
        return jnp.broadcast_to(jnp.sum(v, axis=0, keepdims=True), (8, 128)) * (1.0 / 16.0)

    var = jnp.where(lanes < GROUPS, square * (1.0 / count), 0.0)
    tile = jnp.where(lanes < GROUPS, tile, 0.0)
    mean_all = everywhere(tile)
    gap = tile - mean_all[0:1]
    stats[pl.ds(0, 16)] = tile
    stats[pl.ds(16, 16)] = lax.rsqrt(var + 1e-05)
    stats[pl.ds(32, 8)] = mean_all
    stats[pl.ds(40, 8)] = lax.rsqrt(everywhere(var + gap * gap) + 1e-05)

    for copy in first + second:
        copy.wait_send()


def conv_kernel(
    xd, xn, stats, wl, wd, wgt,
    gam_l, bet_l, bia_l, gam_d, bet_d, bia_d,
    out,
    lhs_d, even, odd, sum_d, sum_l, turn, scale_d, shift_d, scale_l, shift_l,
):
    row = lax.axis_index("row")
    col = lax.axis_index("col")
    has_up = row > 0
    has_dn = row < NROW - 1
    has_lf = col > 0
    has_rt = col < NCOL - 1

    spread = exact_dot(stats[...], lanes_to_channels())
    for n, gam, bet, scale, shift in (
        (0, gam_d, bet_d, scale_d, shift_d), (32, gam_l, bet_l, scale_l, shift_l)
    ):
        rows = 16 if n == 0 else 8
        by = spread[n + rows : n + 2 * rows] * (gam[...].reshape(1, CH) * 0.5)
        scale[...] = by
        shift[...] = bet[...].reshape(1, CH) * 0.5 - spread[n : n + rows] * by

    def silu(x, scale, shift):
        h = x * scale + shift
        return h + h * jnp.tanh(h)

    def mix(d0, d1, d2, d3):
        return (d0 - d2, d1 + d2, d2 - d1, d1 - d3)

    @pl.loop(0, STEPS + 2)
    def _(j):
        for ct in range(5):
            lanes = pl.ds(ct * 128, 128)
            by, plus = scale_d[:, lanes], shift_d[:, lanes]

            def unit(u):
                return silu(xd[u, j, :, lanes].astype(F32), by, plus)

            d0 = jnp.where(has_up, unit(0), 0.0)
            d1 = unit(1)
            for n in range(UNITS // 2):
                d2 = unit(2 * n + 2)
                d3 = unit(2 * n + 3)
                if n == UNITS // 2 - 1:
                    d3 = jnp.where(has_dn, d3, 0.0)
                for k, v in enumerate(mix(d0, d1, d2, d3)):
                    lhs_d[k, n, j, :, lanes] = v.astype(BF16)
                d0, d1 = d2, d3

    for j, ok in ((0, has_lf), (STEPS + 1, has_rt)):
        @pl.when(jnp.logical_not(ok))
        def _():
            for k in range(4):
                for n in range(UNITS // 2):
                    lhs_d[k, n, j] = jnp.zeros((16, CH), BF16)

    sub = lax.broadcasted_iota(jnp.int32, (8, 128), 0)
    keep_lf = (sub > 0) | has_lf
    keep_rt = (sub < 7) | has_rt
    for ct in range(5):
        lanes = pl.ds(ct * 128, 128)
        by, plus = scale_l[:, lanes], shift_l[:, lanes]

        def line(r):
            cells = [silu(xn[ct, r, pl.ds(7 + m, 8, stride=4), :], by, plus) for m in range(6)]
            cells[0] = jnp.where(keep_lf, cells[0], 0.0)
            cells[5] = jnp.where(keep_rt, cells[5], 0.0)
            return cells

        def pair(t, carry):
            d0, d1 = carry[:6], carry[6:]
            d2 = line(2 * t + 2)
            keep = (t < PAIRS - 1) | has_dn
            d3 = [jnp.where(keep, v, 0.0) for v in line(2 * t + 3)]
            mixed = [mix(*quad) for quad in zip(d0, d1, d2, d3)]
            for k in range(4):
                for half in range(3):
                    v = jnp.concatenate([mixed[2 * half][k], mixed[2 * half + 1][k]], axis=0)
                    even[k, t, pl.ds(16 * half, 16), lanes] = v.astype(BF16)
                for half in range(2):
                    v = jnp.concatenate([mixed[2 * half + 1][k], mixed[2 * half + 2][k]], axis=0)
                    odd[k, t, pl.ds(16 * half, 16), lanes] = v.astype(BF16)
            return tuple(d2) + tuple(d3)

        start = tuple(jnp.where(has_up, v, 0.0) for v in line(0)) + tuple(line(1))
        lax.fori_loop(0, PAIRS, pair, start)

    size = PAIRS * COLS

    def products(get, planes, bias, total, n, width):
        at = pl.ds(n, width)
        for k in range(4):
            m = jnp.dot(get(k), planes[k, :, at], preferred_element_type=F32)
            for c in range(width // 128):
                ct = n // 128 + c
                v = m[:, c * 128 : c * 128 + 128]
                if k == 0:
                    total[0, ct] = v + bias[pl.ds(ct * 128, 128)].reshape(1, 128)
                elif k == 1:
                    total[0, ct] += v
                    total[1, ct] = v + bias[pl.ds(ct * 128, 128)].reshape(1, 128)
                elif k == 2:
                    total[0, ct] += v
                    total[1, ct] -= v
                else:
                    total[1, ct] -= v

    def dilated_lhs(k):
        return jnp.concatenate(
            [lhs_d[k, :, b : b + STEPS].reshape(size, CH) for b in range(3)], axis=1
        )

    def local_lhs(k):
        return jnp.concatenate(
            [
                even[k, :, 0:32].reshape(size, CH),
                odd[k].reshape(size, CH),
                even[k, :, 16:48].reshape(size, CH),
            ],
            axis=1,
        )

    chunks = ((0, 256), (256, 256), (512, 128))
    for n, width in chunks:
        products(dilated_lhs, wd, bia_d, sum_d, n, width)
    lower = sub < 4
    for n, width in chunks:
        products(local_lhs, wl, bia_l, sum_l, n, width)

        @pl.loop(0, UNITS // 2)
        def _(g):
            for h in range(2):
                for c in range(width // 128):
                    ct = n // 128 + c
                    lanes = pl.ds(ct * 128, 128)
                    for p in range(4):
                        at = (4 * g + 2 * h + p // 2) * COLS
                        for m in range(4):
                            cells = pl.ds(pl.multiple_of(at + 8 * m, 8), 8)
                            turn[p, pl.ds(m, 8, stride=4), :] = sum_l[p % 2, ct, cells, :]
                    for e in range(2):
                        parts = []
                        for j in range(STEPS):
                            cells = pl.ds(pl.multiple_of((g * STEPS + j) * 16 + 8 * e, 8), 8)
                            parts.append(sum_d[h, ct, cells, :].astype(BF16).astype(F32))
                        for f in range(2):
                            p = 2 * e + f
                            r = 8 * g + 4 * h + p
                            line = []
                            for v in range(4):
                                a, b = parts[2 * v], parts[2 * v + 1]
                                if f == 0:
                                    line.append(jnp.where(lower, a, pltpu.roll(b, 4, 0)))
                                else:
                                    line.append(jnp.where(lower, pltpu.roll(a, 4, 0), b))
                            dil = jnp.concatenate(line, axis=0)
                            w = wgt[pl.ds(pl.multiple_of(r * COLS, COLS), COLS), :]
                            mixed = w * turn[p] + (1.0 - w) * dil
                            out[r, :, lanes] = mixed.astype(BF16)


VM = pl.BlockSpec(memory_space=pltpu.VMEM)
HB = pl.BlockSpec(memory_space=pltpu.HBM)


def per_device(
    latent, blend, gamma_local, beta_local, kernel_local, bias_local,
    gamma_dilated, beta_dilated, kernel_dilated, bias_dilated,
):
    kl = pltpu.with_memory_space_constraint(kernel_local.reshape(3, KDIM, CH), pltpu.HBM)
    kd = pltpu.with_memory_space_constraint(kernel_dilated.reshape(3, KDIM, CH), pltpu.HBM)
    latent = pltpu.with_memory_space_constraint(latent, pltpu.HBM)
    blend = pltpu.with_memory_space_constraint(blend.T, pltpu.HBM)
    dma = pltpu.SemaphoreType.DMA
    gathered = pl.pallas_call(
        gather_kernel,
        out_shape=(
            pltpu.VMEM((UNITS + 2, STEPS + 2, 16, CH), BF16),
            pltpu.VMEM((5, ROWS + 2, 48, 128), F32),
            pltpu.VMEM((48, 128), F32),
            pltpu.VMEM((4, KDIM, CH), BF16),
            pltpu.VMEM((4, KDIM, CH), BF16),
            pltpu.VMEM((ROWS * COLS, 128), F32),
        ),
        in_specs=[HB, HB, HB, HB],
        out_specs=(VM,) * 6,
        scratch_shapes=[
            pltpu.VMEM((ROWS, COLS, CH), BF16),
            pltpu.VMEM((COLS, ROWS), jnp.int32),
            pltpu.VMEM((KDIM, CH), BF16),
            pltpu.VMEM((KDIM, CH), BF16),
            pltpu.VMEM((16, 128), F32),
            pltpu.VMEM((16, 128), F32),
            pltpu.VMEM((NROW, 16, 128), F32),
            pltpu.VMEM((NCOL, 16, 128), F32),
            dma, dma, dma((6,)), dma((8,)), dma((8,)),
            dma((NROW,)), dma((NROW,)), dma((NCOL,)), dma((NCOL,)),
        ],
        compiler_params=pltpu.CompilerParams(
            collective_id=0, has_side_effects=True, vmem_limit_bytes=12 * 2**20
        ),
        name="gather",
    )(latent, kl, kd, blend)
    gathered = [pltpu.with_memory_space_constraint(a, pltpu.VMEM) for a in gathered]
    small = (gamma_local, beta_local, bias_local, gamma_dilated, beta_dilated, bias_dilated)
    return pl.pallas_call(
        conv_kernel,
        out_shape=jax.ShapeDtypeStruct((ROWS, COLS, CH), BF16),
        in_specs=[VM] * 12,
        out_specs=VM,
        scratch_shapes=[
            pltpu.VMEM((4, UNITS // 2, STEPS + 2, 16, CH), BF16),
            pltpu.VMEM((4, PAIRS, 48, CH), BF16),
            pltpu.VMEM((4, PAIRS, 32, CH), BF16),
            pltpu.VMEM((2, 5, PAIRS * COLS, 128), F32),
            pltpu.VMEM((2, 5, PAIRS * COLS, 128), F32),
            pltpu.VMEM((4, COLS, 128), F32),
            pltpu.VMEM((16, CH), F32),
            pltpu.VMEM((16, CH), F32),
            pltpu.VMEM((8, CH), F32),
            pltpu.VMEM((8, CH), F32),
        ],
        compiler_params=pltpu.CompilerParams(vmem_limit_bytes=30 * 2**20),
        name="conv",
    )(*gathered, *small)


def solution(mesh):
    placed = (P("row", "col", None), P("row", "col"), P(), P(), P(), P(), P(), P(), P(), P())
    return jax.shard_map(
        per_device, mesh=mesh, in_specs=placed, out_specs=P("row", "col", None), check_vma=False
    )
```

time: 79 us -> 60.8 us (0.77)
  Pallas kernels: 62.3 us -> 52.4 us
  local copies, waits for them, and re-layouts: 16.2 us -> 7.58 us
    pallas_call x1, Pallas kernels: 38.2 us -> 29 us  [per_device(): pl.pallas_call(conv_kernel, out_shape=jax.ShapeDtypeStruct((ROWS, COLS, C...]
    reshape x6 -> x0, local copies, waits for them, and re-layouts: 7.65 us -> none  [per_device(): a.reshape(1, CH)]
    unnamed x7 -> x4, local copies, waits for them, and re-layouts: 8.52 us -> 7.58 us
where the time goes in v2:
time: 60.8 us; the launch traced here: 59.9 us
  Pallas kernels  52.4 us (86%)
  local copies, waits for them, and re-layouts  7.58 us (12%)
    pallas_call x1, Pallas kernels, per_device(): pl.pallas_call(conv_kernel, out_shape=jax.ShapeDtypeStruct((ROWS, COLS, C...  29 us
    pallas_call x1, Pallas kernels, per_device(): pl.pallas_call(gather_kernel, out_shape=(pltpu.VMEM((UNITS + 2, STEPS + 2...  23.4 us
    unnamed x4, local copies, waits for them, and re-layouts  7.58 us

profile of v2, /device:TPU:1, one launch (start us, length us, event | category | flops | bytes accessed | tf_op | source)
XLA Modules:
  0.0 59.9 jit_solution(8629066713326497769)
XLA Ops:
  0.0 23.4 %gather.1 = (bf16[14,10,16,640]{3,2,1,0:T(8,128)(2,1)S(1)}, f32[5,50,48,128]{3,2,1,0:T(8,128)S(1)}, f32[48,128]{1,0:T(8,128)S(1)}, bf16[4,1920,640]{2,1,0:T(8,12...) custom-call(bf16[48,32,640]{2,1,0:T(8,128)(2,1)} %lat_hbm.1, bf16[3,1920,640]{2,1,0:T(8,128)(2,1)} %bitcast.3, ...), custom_call_target="tpu_custom_call" | custom-call | tf_op jit(solution)/shard_map/gather/pallas_call | solution.py:419
  23.4 0.0 copy-start
  23.4 3.8 %copy-done = bf16[4,1920,640]{2,1,0:T(8,128)(2,1)} copy-done((bf16[4,1920,640]{2,1,0:T(8,128)(2,1)}, bf16[4,1920,640]{2,1,0:T(8,128)(2,1)S(1)}, u32[]{:S(2)}) %copy-start) | copy-done | bytes 9830424
  27.2 0.0 copy-start.1
  27.2 3.8 %copy-done.1 = bf16[4,1920,640]{2,1,0:T(8,128)(2,1)S(1)} copy-done((bf16[4,1920,640]{2,1,0:T(8,128)(2,1)S(1)}, bf16[4,1920,640]{2,1,0:T(8,128)(2,1)}, u32[]{:S(2)}) %copy-start.1) | copy-done | bytes 9830424
  31.0 29.0 %conv.1 = bf16[48,32,640]{2,1,0:T(8,128)(2,1)} custom-call(bf16[14,10,16,640]{3,2,1,0:T(8,128)(2,1)S(1)} %get-tuple-element.11.xd, f32[5,50,48,128]{3,2,1,0:T(8,128)S(1)} %get-tuple-element.12.xn, f32[48,128]{1,0:T(8,128)S(1)} %get-tuple-element.13.stats, bf16[4,1920,640]{2,1,0:T(8,128)(2,1)S(1)} %copy-done.1, ...), custom_call_target="tpu_custom_call" | custom-call | tf_op jit(solution)/shard_map/conv/pallas_call | solution.py:450
Async XLA Ops:
  23.4 3.8 %copy-start = (bf16[4,1920,640]{2,1,0:T(8,128)(2,1)}, bf16[4,1920,640]{2,1,0:T(8,128)(2,1)S(1)}, u32[]{:S(2)}) copy-start(bf16[4,1920,640]{2,1,0:T(8,128)(2,1)S(1)} %get-tuple-element.14.wl) | copy-start | bytes 29491204
  27.2 3.8 %copy-start.1 = (bf16[4,1920,640]{2,1,0:T(8,128)(2,1)S(1)}, bf16[4,1920,640]{2,1,0:T(8,128)(2,1)}, u32[]{:S(2)}) copy-start(bf16[4,1920,640]{2,1,0:T(8,128)(2,1)} %copy-done) | copy-start | bytes 29491204

commit v3 on v2

--- a/solution.py
+++ b/solution.py
@@ -19,6 +19,7 @@
 NCOL = 16
 UNITS = ROWS // 4
 STEPS = COLS // 4
+PARTS = 4
 LOCAL_COUNT = float(UNITS * STEPS * PER_GROUP)
 
 
@@ -70,16 +71,14 @@
     has_lf = col > 0
     has_rt = col < NCOL - 1
 
-    load = pltpu.make_async_copy(lat_hbm, lat, sem_in)
-    load.start()
+    loads = []
+    for n in range(PARTS):
+        at = pl.ds(n * (ROWS // PARTS), ROWS // PARTS)
+        copy = pltpu.make_async_copy(lat_hbm.at[at], lat.at[at], sem_in.at[n])
+        copy.start()
+        loads.append(copy)
     load_blend = pltpu.make_async_copy(blend_hbm, blend_ref, sem_b)
     load_blend.start()
-    weights = []
-    for n, (src, planes, mid) in enumerate(((kd_hbm, wd, mid_d), (kl_hbm, wl, mid_l))):
-        for m, (a, dst) in enumerate(((0, planes.at[0]), (1, mid), (2, planes.at[3]))):
-            copy = pltpu.make_async_copy(src.at[a], dst, sem_w.at[3 * n + m])
-            copy.start()
-            weights.append(copy)
 
     barrier = pltpu.get_barrier_semaphore()
     for d in range(1, NROW):
@@ -92,9 +91,16 @@
             def _():
                 pl.semaphore_signal(barrier, 1, device_id=(row + dr, col + dc), device_id_type=MESH)
 
-    load.wait()
-
-    def arrange(u, acc):
+    loads[0].wait()
+    cells = jnp.concatenate([lat[p, 0:16, :].astype(F32)[0:4] for p in range(4)], axis=0)
+    centre = jnp.dot(
+        cells.astype(BF16), groups_to_lanes(0).astype(BF16), preferred_element_type=F32
+    )
+    centre = (centre * (1.0 / PER_GROUP)).astype(BF16)
+    shift = jnp.dot(centre, lanes_to_channels().astype(BF16), preferred_element_type=F32)
+
+    def arrange(u, carry):
+        acc, square = carry
         rows = []
         for p in range(4):
             x = lat[4 * u + p].astype(F32)
@@ -103,22 +109,29 @@
             rows.append(x)
         for j in range(STEPS):
             cells = jnp.concatenate([x[4 * j : 4 * j + 4] for x in rows], axis=0)
-            acc = acc + cells
             xd[u + 1, j + 1] = cells.astype(BF16)
-        return acc
-
-    acc = lax.fori_loop(0, UNITS, arrange, jnp.zeros((16, CH), F32))
-    mean = exact_dot(acc, groups_to_lanes(0)) * (1.0 / LOCAL_COUNT)
-    centre = exact_dot(mean, lanes_to_channels())
-
-    def squares(u, acc):
-        for j in range(STEPS):
-            gap = xd[u + 1, j + 1].astype(F32) - centre
-            acc = acc + gap * gap
-        return acc
-
-    acc = lax.fori_loop(0, UNITS, squares, jnp.zeros((16, CH), F32))
-    square = exact_dot(acc, groups_to_lanes(GROUPS))
+            gap = cells - shift
+            acc = acc + gap
+            square = square + gap * gap
+        return acc, square
+
+    carry = (jnp.zeros((16, CH), F32), jnp.zeros((16, CH), F32))
+    for n in range(PARTS):
+        if n:
+            loads[n].wait()
+        carry = lax.fori_loop(n * UNITS // PARTS, (n + 1) * UNITS // PARTS, arrange, carry)
+
+    weights = []
+    for n, (src, planes, mid) in enumerate(((kd_hbm, wd, mid_d), (kl_hbm, wl, mid_l))):
+        for m, (a, dst) in enumerate(((0, planes.at[0]), (1, mid), (2, planes.at[3]))):
+            copy = pltpu.make_async_copy(src.at[a], dst, sem_w.at[3 * n + m])
+            copy.start()
+            weights.append(copy)
+
+    gap = exact_dot(carry[0], groups_to_lanes(0))
+    square = exact_dot(carry[1], groups_to_lanes(GROUPS))
+    mean = centre.astype(F32) + gap * (1.0 / LOCAL_COUNT)
+    square = square - pltpu.roll(gap * gap, GROUPS, 1) * (1.0 / LOCAL_COUNT)
     lanes = lax.broadcasted_iota(jnp.int32, (16, 128), 1)
     tile1[...] = jnp.where(lanes < GROUPS, mean, square)
 
@@ -157,7 +170,7 @@
         def _():
             copy.start()
 
-    def planes(dst, mid):
+    def form(dst, mid):
         @pl.loop(0, KDIM // 32)
         def _(i):
             at = pl.ds(pl.multiple_of(i * 32, 32), 32)
@@ -185,10 +198,10 @@
 
     for copy in weights[:3]:
         copy.wait()
-    planes(wd, mid_d)
+    form(wd, mid_d)
     for copy in weights[3:]:
         copy.wait()
-    planes(wl, mid_l)
+    form(wl, mid_l)
 
     for copy, ok, got in halos:
         @pl.when(got)
@@ -246,7 +259,7 @@
     xd, xn, stats, wl, wd, wgt,
     gam_l, bet_l, bia_l, gam_d, bet_d, bia_d,
     out,
-    lhs_d, even, odd, sum_d, sum_l, turn, scale_d, shift_d, scale_l, shift_l,
+    lhs_d, even, odd, sum_d, total, turn, scale_d, shift_d, scale_l, shift_l,
 ):
     row = lax.axis_index("row")
     col = lax.axis_index("col")
@@ -331,7 +344,7 @@
 
     size = PAIRS * COLS
 
-    def products(get, planes, bias, total, n, width):
+    def products(get, planes, bias, n, width, keep):
         at = pl.ds(n, width)
         for k in range(4):
             m = jnp.dot(get(k), planes[k, :, at], preferred_element_type=F32)
@@ -339,15 +352,21 @@
                 ct = n // 128 + c
                 v = m[:, c * 128 : c * 128 + 128]
                 if k == 0:
-                    total[0, ct] = v + bias[pl.ds(ct * 128, 128)].reshape(1, 128)
+                    total[0, c] = v + bias[pl.ds(ct * 128, 128)].reshape(1, 128)
                 elif k == 1:
-                    total[0, ct] += v
-                    total[1, ct] = v + bias[pl.ds(ct * 128, 128)].reshape(1, 128)
+                    total[0, c] += v
+                    total[1, c] = v + bias[pl.ds(ct * 128, 128)].reshape(1, 128)
                 elif k == 2:
-                    total[0, ct] += v
-                    total[1, ct] -= v
+                    keep(0, c, ct, total[0, c] + v)
+                    total[1, c] -= v
                 else:
-                    total[1, ct] -= v
+                    keep(1, c, ct, total[1, c] - v)
+
+    def keep_dilated(h, c, ct, v):
+        sum_d[h, ct] = v.astype(BF16)
+
+    def keep_local(h, c, ct, v):
+        total[h, c] = v
 
     def dilated_lhs(k):
         return jnp.concatenate(
@@ -364,12 +383,12 @@
             axis=1,
         )
 
-    chunks = ((0, 256), (256, 256), (512, 128))
+    chunks = ((0, 512), (512, 128))
     for n, width in chunks:
-        products(dilated_lhs, wd, bia_d, sum_d, n, width)
+        products(dilated_lhs, wd, bia_d, n, width, keep_dilated)
     lower = sub < 4
     for n, width in chunks:
-        products(local_lhs, wl, bia_l, sum_l, n, width)
+        products(local_lhs, wl, bia_l, n, width, keep_local)
 
         @pl.loop(0, UNITS // 2)
         def _(g):
@@ -381,12 +400,13 @@
                         at = (4 * g + 2 * h + p // 2) * COLS
                         for m in range(4):
                             cells = pl.ds(pl.multiple_of(at + 8 * m, 8), 8)
-                            turn[p, pl.ds(m, 8, stride=4), :] = sum_l[p % 2, ct, cells, :]
+                            turn[p, pl.ds(m, 8, stride=4), :] = total[p % 2, c, cells, :]
+                    whole = []
+                    for j in range(STEPS):
+                        cells = pl.ds(pl.multiple_of((g * STEPS + j) * 16, 16), 16)
+                        whole.append(sum_d[h, ct, cells, :].astype(F32))
                     for e in range(2):
-                        parts = []
-                        for j in range(STEPS):
-                            cells = pl.ds(pl.multiple_of((g * STEPS + j) * 16 + 8 * e, 8), 8)
-                            parts.append(sum_d[h, ct, cells, :].astype(BF16).astype(F32))
+                        parts = [x[8 * e : 8 * e + 8] for x in whole]
                         for f in range(2):
                             p = 2 * e + f
                             r = 8 * g + 4 * h + p
@@ -437,7 +457,7 @@
             pltpu.VMEM((16, 128), F32),
             pltpu.VMEM((NROW, 16, 128), F32),
             pltpu.VMEM((NCOL, 16, 128), F32),
-            dma, dma, dma((6,)), dma((8,)), dma((8,)),
+            dma((PARTS,)), dma, dma((6,)), dma((8,)), dma((8,)),
             dma((NROW,)), dma((NROW,)), dma((NCOL,)), dma((NCOL,)),
         ],
         compiler_params=pltpu.CompilerParams(
@@ -456,15 +476,15 @@
             pltpu.VMEM((4, UNITS // 2, STEPS + 2, 16, CH), BF16),
             pltpu.VMEM((4, PAIRS, 48, CH), BF16),
             pltpu.VMEM((4, PAIRS, 32, CH), BF16),
-            pltpu.VMEM((2, 5, PAIRS * COLS, 128), F32),
-            pltpu.VMEM((2, 5, PAIRS * COLS, 128), F32),
+            pltpu.VMEM((2, 5, PAIRS * COLS, 128), BF16),
+            pltpu.VMEM((2, 4, PAIRS * COLS, 128), F32),
             pltpu.VMEM((4, COLS, 128), F32),
             pltpu.VMEM((16, CH), F32),
             pltpu.VMEM((16, CH), F32),
             pltpu.VMEM((8, CH), F32),
             pltpu.VMEM((8, CH), F32),
         ],
-        compiler_params=pltpu.CompilerParams(vmem_limit_bytes=30 * 2**20),
+        compiler_params=pltpu.CompilerParams(vmem_limit_bytes=25 * 2**20),
         name="conv",
     )(*gathered, *small)
 

time: 60.8 us -> 47.9 us (0.79)
  local copies, waits for them, and re-layouts: 7.58 us -> 0.02 us
  Pallas kernels: 52.4 us -> 47 us
    unnamed x4 -> x12, local copies, waits for them, and re-layouts: 7.58 us -> 0.02 us
    pallas_call x1, Pallas kernels: 23.4 us -> 19.1 us  [per_device(): pl.pallas_call(gather_kernel, out_shape=(pltpu.VMEM((UNITS + 2, STEPS + 2...]
    pallas_call x1, Pallas kernels: 29 us -> 28 us  [per_device(): pl.pallas_call(conv_kernel, out_shape=jax.ShapeDtypeStruct((ROWS, COLS, C...]
where the time goes in v3:
time: 47.9 us; the launch traced here: 47.2 us
  Pallas kernels  47 us (98%)
    pallas_call x1, Pallas kernels, per_device(): pl.pallas_call(conv_kernel, out_shape=jax.ShapeDtypeStruct((ROWS, COLS, C...  28 us
    pallas_call x1, Pallas kernels, per_device(): pl.pallas_call(gather_kernel, out_shape=(pltpu.VMEM((UNITS + 2, STEPS + 2...  19.1 us

profile of v3, /device:TPU:1, one launch (start us, length us, event | category | flops | bytes accessed | tf_op | source)
XLA Modules:
  0.0 47.2 jit_solution(5754930931447280109)
XLA Ops:
  0.0 0.0 copy-start
  0.0 0.0 copy-start.1
  0.0 0.0 copy-start.2
  0.0 0.0 copy-start.3
  0.0 0.0 copy-start.4
  0.0 0.0 copy-start.5
  0.0 19.1 %gather.1 = (bf16[14,10,16,640]{3,2,1,0:T(8,128)(2,1)S(1)}, f32[5,50,48,128]{3,2,1,0:T(8,128)S(1)}, f32[48,128]{1,0:T(8,128)S(1)}, bf16[4,1920,640]{2,1,0:T(8,12...) custom-call(bf16[48,32,640]{2,1,0:T(8,128)(2,1)} %lat_hbm.1, bf16[3,1920,640]{2,1,0:T(8,128)(2,1)} %bitcast.3, ...), custom_call_target="tpu_custom_call" | custom-call | tf_op jit(solution)/shard_map/gather/pallas_call | solution.py:439
  19.1 0.0 copy-done
  19.1 0.0 copy-done.1
  19.1 0.0 copy-done.2
  19.2 0.0 copy-done.3
  19.2 0.0 copy-done.4
  19.2 0.0 copy-done.5
  19.2 28.0 %conv.1 = bf16[48,32,640]{2,1,0:T(8,128)(2,1)} custom-call(bf16[14,10,16,640]{3,2,1,0:T(8,128)(2,1)S(1)} %get-tuple-element.11.xd, f32[5,50,48,128]{3,2,1,0:T(8,128)S(1)} %get-tuple-element.12.xn, f32[48,128]{1,0:T(8,128)S(1)} %get-tuple-element.13.stats, bf16[4,1920,640]{2,1,0:T(8,128)(2,1)S(1)} %get-tuple-element.14.wl, ...), custom_call_target="tpu_custom_call" | custom-call | tf_op jit(solution)/shard_map/conv/pallas_call | solution.py:470
Async XLA Ops:
  0.0 19.1 %copy-start = (f32[640]{0:T(1024)S(1)}, f32[640]{0:T(1024)}, u32[]{:S(2)}) copy-start(f32[640]{0:T(1024)} %gam_l.1) | copy-start | bytes 7684
  0.0 19.1 %copy-start.1 = (f32[640]{0:T(1024)S(1)}, f32[640]{0:T(1024)}, u32[]{:S(2)}) copy-start(f32[640]{0:T(1024)} %bet_l.1) | copy-start | bytes 7684
  0.0 19.1 %copy-start.2 = (f32[640]{0:T(1024)S(1)}, f32[640]{0:T(1024)}, u32[]{:S(2)}) copy-start(f32[640]{0:T(1024)} %bia_l.1) | copy-start | bytes 7684
  0.0 19.2 %copy-start.3 = (f32[640]{0:T(1024)S(1)}, f32[640]{0:T(1024)}, u32[]{:S(2)}) copy-start(f32[640]{0:T(1024)} %gam_d.1) | copy-start | bytes 7684
  0.0 19.2 %copy-start.4 = (f32[640]{0:T(1024)S(1)}, f32[640]{0:T(1024)}, u32[]{:S(2)}) copy-start(f32[640]{0:T(1024)} %bet_d.1) | copy-start | bytes 7684
  0.0 19.2 %copy-start.5 = (f32[640]{0:T(1024)S(1)}, f32[640]{0:T(1024)}, u32[]{:S(2)}) copy-start(f32[640]{0:T(1024)} %bia_d.1) | copy-start | bytes 7684

commit v4 on v3

--- a/solution.py
+++ b/solution.py
@@ -19,6 +19,7 @@
 NCOL = 16
 UNITS = ROWS // 4
 STEPS = COLS // 4
+BLOCKS = (UNITS // 2) * (STEPS + 2)
 PARTS = 4
 LOCAL_COUNT = float(UNITS * STEPS * PER_GROUP)
 
@@ -105,7 +106,7 @@
         for p in range(4):
             x = lat[4 * u + p].astype(F32)
             for ct in range(5):
-                xn[ct, 4 * u + p + 1, pl.ds(8, COLS), :] = x[:, ct * 128 : ct * 128 + 128]
+                xn[ct, 4 * u + p + 1, pl.ds(0, COLS), :] = x[:, ct * 128 : ct * 128 + 128]
             rows.append(x)
         for j in range(STEPS):
             cells = jnp.concatenate([x[4 * j : 4 * j + 4] for x in rows], axis=0)
@@ -182,7 +183,7 @@
     load_blend.wait()
     turned = blend_ref[...].astype(F32) * 0.25
     for r in range(ROWS):
-        wgt[pl.ds(r * COLS, COLS), :] = jnp.broadcast_to(turned[:, r : r + 1], (COLS, 128))
+        wgt[pl.ds(r * COLS, COLS), :] = jnp.broadcast_to(turned[:, r : r + 1], (COLS, 128)).astype(BF16)
 
     for copy in first:
         copy.wait_recv()
@@ -217,8 +218,8 @@
         for j in range(STEPS):
             x = xd[src, j + 1].astype(F32)[part : part + 4]
             for ct in range(5):
-                xn[ct, at, pl.ds(8 + 4 * j, 4), :] = x[:, ct * 128 : ct * 128 + 128]
-    for j, q, at in ((0, 3, 7), (STEPS + 1, 0, 8 + COLS)):
+                xn[ct, at, pl.ds(4 * j, 4), :] = x[:, ct * 128 : ct * 128 + 128]
+    for j, q, at in ((0, 3, COLS + 1), (STEPS + 1, 0, COLS)):
         @pl.loop(0, UNITS)
         def _(u):
             x = xd[u + 1, j].astype(F32)
@@ -259,7 +260,8 @@
     xd, xn, stats, wl, wd, wgt,
     gam_l, bet_l, bia_l, gam_d, bet_d, bia_d,
     out,
-    lhs_d, even, odd, sum_d, total, turn, scale_d, shift_d, scale_l, shift_l,
+    lhs_d, even, odd, sum_d, total_a, total_b, turn, scale_d, shift_d, scale_l, shift_l,
+    sem_a, sem_b,
 ):
     row = lax.axis_index("row")
     col = lax.axis_index("col")
@@ -301,7 +303,7 @@
                 if n == UNITS // 2 - 1:
                     d3 = jnp.where(has_dn, d3, 0.0)
                 for k, v in enumerate(mix(d0, d1, d2, d3)):
-                    lhs_d[k, n, j, :, lanes] = v.astype(BF16)
+                    lhs_d[k * BLOCKS + n * (STEPS + 2) + j, :, lanes] = v.astype(BF16)
                 d0, d1 = d2, d3
 
     for j, ok in ((0, has_lf), (STEPS + 1, has_rt)):
@@ -309,45 +311,50 @@
         def _():
             for k in range(4):
                 for n in range(UNITS // 2):
-                    lhs_d[k, n, j] = jnp.zeros((16, CH), BF16)
+                    lhs_d[k * BLOCKS + n * (STEPS + 2) + j] = jnp.zeros((16, CH), BF16)
 
     sub = lax.broadcasted_iota(jnp.int32, (8, 128), 0)
-    keep_lf = (sub > 0) | has_lf
+    first = sub == 0
     keep_rt = (sub < 7) | has_rt
-    for ct in range(5):
-        lanes = pl.ds(ct * 128, 128)
-        by, plus = scale_l[:, lanes], shift_l[:, lanes]
-
-        def line(r):
-            cells = [silu(xn[ct, r, pl.ds(7 + m, 8, stride=4), :], by, plus) for m in range(6)]
-            cells[0] = jnp.where(keep_lf, cells[0], 0.0)
-            cells[5] = jnp.where(keep_rt, cells[5], 0.0)
-            return cells
-
-        def pair(t, carry):
-            d0, d1 = carry[:6], carry[6:]
-            d2 = line(2 * t + 2)
-            keep = (t < PAIRS - 1) | has_dn
-            d3 = [jnp.where(keep, v, 0.0) for v in line(2 * t + 3)]
-            mixed = [mix(*quad) for quad in zip(d0, d1, d2, d3)]
-            for k in range(4):
-                for half in range(3):
-                    v = jnp.concatenate([mixed[2 * half][k], mixed[2 * half + 1][k]], axis=0)
-                    even[k, t, pl.ds(16 * half, 16), lanes] = v.astype(BF16)
-                for half in range(2):
-                    v = jnp.concatenate([mixed[2 * half + 1][k], mixed[2 * half + 2][k]], axis=0)
-                    odd[k, t, pl.ds(16 * half, 16), lanes] = v.astype(BF16)
-            return tuple(d2) + tuple(d3)
-
-        start = tuple(jnp.where(has_up, v, 0.0) for v in line(0)) + tuple(line(1))
-        lax.fori_loop(0, PAIRS, pair, start)
+
+    def form_local(t0, t1):
+        for ct in range(5):
+            lanes = pl.ds(ct * 128, 128)
+            by, plus = scale_l[:, lanes], shift_l[:, lanes]
+
+            def line(r):
+                cells = [silu(xn[ct, r, pl.ds(m, 8, stride=4), :], by, plus) for m in range(5)]
+                cells[4] = jnp.where(keep_rt, cells[4], 0.0)
+                edge = silu(jnp.broadcast_to(xn[ct, r, pl.ds(COLS + 1, 1), :], (8, 128)), by, plus)
+                edge = jnp.where(has_lf, edge, 0.0)
+                cells.insert(0, jnp.where(first, edge, pltpu.roll(cells[3], 1, 0)))
+                if r == 0:
+                    cells = [jnp.where(has_up, v, 0.0) for v in cells]
+                if r == ROWS + 1:
+                    cells = [jnp.where(has_dn, v, 0.0) for v in cells]
+                return cells
+
+            d0, d1 = line(2 * t0), line(2 * t0 + 1)
+            for t in range(t0, t1):
+                d2, d3 = line(2 * t + 2), line(2 * t + 3)
+                mixed = [mix(*quad) for quad in zip(d0, d1, d2, d3)]
+                for k in range(4):
+                    for half in range(3):
+                        v = jnp.concatenate([mixed[2 * half][k], mixed[2 * half + 1][k]], axis=0)
+                        even[k, t, pl.ds(16 * half, 16), lanes] = v.astype(BF16)
+                    for half in range(2):
+                        v = jnp.concatenate([mixed[2 * half + 1][k], mixed[2 * half + 2][k]], axis=0)
+                        odd[k, t, pl.ds(16 * half, 16), lanes] = v.astype(BF16)
+                d0, d1 = d2, d3
 
     size = PAIRS * COLS
 
-    def products(get, planes, bias, n, width, keep):
+    def products(get, planes, bias, n, width, total, keep, beside=None):
         at = pl.ds(n, width)
         for k in range(4):
             m = jnp.dot(get(k), planes[k, :, at], preferred_element_type=F32)
+            if beside is not None:
+                beside(k)
             for c in range(width // 128):
                 ct = n // 128 + c
                 v = m[:, c * 128 : c * 128 + 128]
@@ -365,13 +372,20 @@
     def keep_dilated(h, c, ct, v):
         sum_d[h, ct] = v.astype(BF16)
 
-    def keep_local(h, c, ct, v):
-        total[h, c] = v
+    def keep_local(total):
+        def keep(h, c, ct, v):
+            total[h, c] = v
+
+        return keep
 
     def dilated_lhs(k):
-        return jnp.concatenate(
-            [lhs_d[k, :, b : b + STEPS].reshape(size, CH) for b in range(3)], axis=1
-        )
+        taps = []
+        for b in range(3):
+            lines = [
+                lhs_d[pl.ds(k * BLOCKS + n * (STEPS + 2) + b, STEPS)] for n in range(UNITS // 2)
+            ]
+            taps.append(jnp.concatenate(lines, axis=0).reshape(size, CH))
+        return jnp.concatenate(taps, axis=1)
 
     def local_lhs(k):
         return jnp.concatenate(
@@ -383,44 +397,61 @@
             axis=1,
         )
 
-    chunks = ((0, 512), (512, 128))
-    for n, width in chunks:
-        products(dilated_lhs, wd, bia_d, n, width, keep_dilated)
     lower = sub < 4
-    for n, width in chunks:
-        products(local_lhs, wl, bia_l, n, width, keep_local)
-
-        @pl.loop(0, UNITS // 2)
-        def _(g):
-            for h in range(2):
-                for c in range(width // 128):
-                    ct = n // 128 + c
-                    lanes = pl.ds(ct * 128, 128)
-                    for p in range(4):
-                        at = (4 * g + 2 * h + p // 2) * COLS
-                        for m in range(4):
-                            cells = pl.ds(pl.multiple_of(at + 8 * m, 8), 8)
-                            turn[p, pl.ds(m, 8, stride=4), :] = total[p % 2, c, cells, :]
-                    whole = []
-                    for j in range(STEPS):
-                        cells = pl.ds(pl.multiple_of((g * STEPS + j) * 16, 16), 16)
-                        whole.append(sum_d[h, ct, cells, :].astype(F32))
-                    for e in range(2):
-                        parts = [x[8 * e : 8 * e + 8] for x in whole]
-                        for f in range(2):
-                            p = 2 * e + f
-                            r = 8 * g + 4 * h + p
-                            line = []
-                            for v in range(4):
-                                a, b = parts[2 * v], parts[2 * v + 1]
-                                if f == 0:
-                                    line.append(jnp.where(lower, a, pltpu.roll(b, 4, 0)))
-                                else:
-                                    line.append(jnp.where(lower, pltpu.roll(a, 4, 0), b))
-                            dil = jnp.concatenate(line, axis=0)
-                            w = wgt[pl.ds(pl.multiple_of(r * COLS, COLS), COLS), :]
-                            mixed = w * turn[p] + (1.0 - w) * dil
-                            out[r, :, lanes] = mixed.astype(BF16)
+
+    def blend(total, n, width, g, h):
+        for c in range(width // 128):
+            ct = n // 128 + c
+            lanes = pl.ds(ct * 128, 128)
+            for p in range(4):
+                at = (4 * g + 2 * h + p // 2) * COLS
+                for m in range(4):
+                    cells = total[p % 2, c, pl.ds(at + 8 * m, 8), :]
+                    turn[c, h, p, pl.ds(m, 8, stride=4), :] = cells
+            whole = []
+            for j in range(STEPS):
+                whole.append(sum_d[h, ct, pl.ds((g * STEPS + j) * 16, 16), :].astype(F32))
+            for e in range(2):
+                parts = [x[8 * e : 8 * e + 8] for x in whole]
+                for f in range(2):
+                    p = 2 * e + f
+                    r = 8 * g + 4 * h + p
+                    line = []
+                    for v in range(4):
+                        a, b = parts[2 * v], parts[2 * v + 1]
+                        if f == 0:
+                            line.append(jnp.where(lower, a, pltpu.roll(b, 4, 0)))
+                        else:
+                            line.append(jnp.where(lower, pltpu.roll(a, 4, 0), b))
+                    dil = jnp.concatenate(line, axis=0)
+                    w = wgt[pl.ds(r * COLS, COLS), :].astype(F32)
+                    mixed = w * turn[c, h, p] + (1.0 - w) * dil
+                    mixed = mixed.astype(BF16)
+                    lhs_d[2 * r, :, lanes] = mixed[0:16]
+                    lhs_d[2 * r + 1, :, lanes] = mixed[16:32]
+
+    quarter = PAIRS // 4
+    products(
+        dilated_lhs, wd, bia_d, 0, 512, total_a, keep_dilated,
+        lambda k: form_local(k * quarter, (k + 1) * quarter),
+    )
+    products(dilated_lhs, wd, bia_d, 512, 128, total_b, keep_dilated)
+    products(local_lhs, wl, bia_l, 0, 512, total_a, keep_local(total_a))
+
+    def beside(k):
+        for unit in range(3 * k, 3 * k + 3):
+            blend(total_a, 0, 512, unit // 2, unit % 2)
+
+    products(local_lhs, wl, bia_l, 512, 128, total_b, keep_local(total_b), beside)
+    result = lhs_d.at[pl.ds(0, 2 * ROWS)]
+    store_a = pltpu.make_async_copy(result.at[:, :, pl.ds(0, 512)], out.at[:, :, pl.ds(0, 512)], sem_a)
+    store_a.start()
+    for unit in range(UNITS):
+        blend(total_b, 512, 128, unit // 2, unit % 2)
+    store_b = pltpu.make_async_copy(result.at[:, :, pl.ds(512, 128)], out.at[:, :, pl.ds(512, 128)], sem_b)
+    store_b.start()
+    store_a.wait()
+    store_b.wait()
 
 
 VM = pl.BlockSpec(memory_space=pltpu.VMEM)
@@ -440,11 +471,11 @@
         gather_kernel,
         out_shape=(
             pltpu.VMEM((UNITS + 2, STEPS + 2, 16, CH), BF16),
-            pltpu.VMEM((5, ROWS + 2, 48, 128), F32),
+            pltpu.VMEM((5, ROWS + 2, 40, 128), F32),
             pltpu.VMEM((48, 128), F32),
             pltpu.VMEM((4, KDIM, CH), BF16),
             pltpu.VMEM((4, KDIM, CH), BF16),
-            pltpu.VMEM((ROWS * COLS, 128), F32),
+            pltpu.VMEM((ROWS * COLS, 128), BF16),
         ),
         in_specs=[HB, HB, HB, HB],
         out_specs=(VM,) * 6,
@@ -469,24 +500,27 @@
     small = (gamma_local, beta_local, bias_local, gamma_dilated, beta_dilated, bias_dilated)
     return pl.pallas_call(
         conv_kernel,
-        out_shape=jax.ShapeDtypeStruct((ROWS, COLS, CH), BF16),
+        out_shape=jax.ShapeDtypeStruct((2 * ROWS, 16, CH), BF16),
         in_specs=[VM] * 12,
-        out_specs=VM,
+        out_specs=HB,
         scratch_shapes=[
-            pltpu.VMEM((4, UNITS // 2, STEPS + 2, 16, CH), BF16),
+            pltpu.VMEM((4 * BLOCKS, 16, CH), BF16),
             pltpu.VMEM((4, PAIRS, 48, CH), BF16),
             pltpu.VMEM((4, PAIRS, 32, CH), BF16),
             pltpu.VMEM((2, 5, PAIRS * COLS, 128), BF16),
             pltpu.VMEM((2, 4, PAIRS * COLS, 128), F32),
-            pltpu.VMEM((4, COLS, 128), F32),
+            pltpu.VMEM((2, 1, PAIRS * COLS, 128), F32),
+            pltpu.VMEM((4, 2, 4, COLS, 128), F32),
             pltpu.VMEM((16, CH), F32),
             pltpu.VMEM((16, CH), F32),
             pltpu.VMEM((8, CH), F32),
             pltpu.VMEM((8, CH), F32),
+            dma,
+            dma,
         ],
-        compiler_params=pltpu.CompilerParams(vmem_limit_bytes=25 * 2**20),
+        compiler_params=pltpu.CompilerParams(vmem_limit_bytes=26 * 2**20 + 2**18),
         name="conv",
-    )(*gathered, *small)
+    )(*gathered, *small).reshape(ROWS, COLS, CH)
 
 
 def solution(mesh):

time: 47.9 us -> 44.5 us (0.929)
  Pallas kernels: 47 us -> 43.5 us
    pallas_call x1, Pallas kernels: 28 us -> 24.4 us  [per_device(): pl.pallas_call(conv_kernel, out_shape=jax.ShapeDtypeStruct((2 * ROWS, 16,...]
where the time goes in v4:
time: 44.5 us; the launch traced here: 43.8 us
  Pallas kernels  43.5 us (98%)
    pallas_call x1, Pallas kernels, per_device(): pl.pallas_call(conv_kernel, out_shape=jax.ShapeDtypeStruct((2 * ROWS, 16,...  24.4 us
    pallas_call x1, Pallas kernels, per_device(): pl.pallas_call(gather_kernel, out_shape=(pltpu.VMEM((UNITS + 2, STEPS + 2...  19.1 us

profile of v4, /device:TPU:1, one launch (start us, length us, event | category | flops | bytes accessed | tf_op | source)
XLA Modules:
  0.0 43.8 jit_solution(9305844853120095731)
XLA Ops:
  0.0 0.0 copy-start
  0.0 0.0 copy-start.1
  0.0 0.0 copy-start.2
  0.0 0.0 copy-start.3
  0.0 0.0 copy-start.4
  0.0 0.0 copy-start.5
  0.0 19.1 %gather.1 = (bf16[14,10,16,640]{3,2,1,0:T(8,128)(2,1)S(1)}, f32[5,50,40,128]{3,2,1,0:T(8,128)S(1)}, f32[48,128]{1,0:T(8,128)S(1)}, bf16[4,1920,640]{2,1,0:T(8,12...) custom-call(bf16[48,32,640]{2,1,0:T(8,128)(2,1)} %lat_hbm.1, ...), custom_call_target="tpu_custom_call" | custom-call | tf_op jit(solution)/shard_map/gather/pallas_call | solution.py:470
  19.1 0.0 copy-done
  19.1 0.0 copy-done.1
  19.1 0.0 copy-done.2
  19.2 0.0 copy-done.3
  19.2 0.0 copy-done.4
  19.2 0.0 copy-done.5
  19.2 24.4 %conv.1 = bf16[96,16,640]{2,1,0:T(8,128)(2,1)} custom-call(bf16[14,10,16,640]{3,2,1,0:T(8,128)(2,1)S(1)} %get-tuple-element.11.xd, f32[5,50,40,128]{3,2,1,0:T(8,128)S(1)} %get-tuple-element.12.xn, f32[48,128]{1,0:T(8,128)S(1)} %get-tuple-element.13.stats, bf16[4,1920,640]{2,1,0:T(8,128)(2,1)S(1)} %get-tuple-element.14.wl, ...), custom_call_target="tpu_custom_call" | custom-call | tf_op jit(solution)/shard_map/conv/pallas_call | solution.py:501
Async XLA Ops:
  0.0 19.1 %copy-start = (f32[640]{0:T(1024)S(1)}, f32[640]{0:T(1024)}, u32[]{:S(2)}) copy-start(f32[640]{0:T(1024)} %gam_l.1) | copy-start | bytes 7684
  0.0 19.1 %copy-start.1 = (f32[640]{0:T(1024)S(1)}, f32[640]{0:T(1024)}, u32[]{:S(2)}) copy-start(f32[640]{0:T(1024)} %bet_l.1) | copy-start | bytes 7684
  0.0 19.1 %copy-start.2 = (f32[640]{0:T(1024)S(1)}, f32[640]{0:T(1024)}, u32[]{:S(2)}) copy-start(f32[640]{0:T(1024)} %bia_l.1) | copy-start | bytes 7684
  0.0 19.2 %copy-start.3 = (f32[640]{0:T(1024)S(1)}, f32[640]{0:T(1024)}, u32[]{:S(2)}) copy-start(f32[640]{0:T(1024)} %gam_d.1) | copy-start | bytes 7684
  0.0 19.2 %copy-start.4 = (f32[640]{0:T(1024)S(1)}, f32[640]{0:T(1024)}, u32[]{:S(2)}) copy-start(f32[640]{0:T(1024)} %bet_d.1) | copy-start | bytes 7684
  0.0 19.2 %copy-start.5 = (f32[640]{0:T(1024)S(1)}, f32[640]{0:T(1024)}, u32[]{:S(2)}) copy-start(f32[640]{0:T(1024)} %bia_d.1) | copy-start | bytes 7684

commit v5 on v4

--- a/solution.py
+++ b/solution.py
@@ -55,8 +55,9 @@
     for tile in tiles:
         gap = tile - average
         spread = gap * gap if spread is None else spread + gap * gap
-    lanes = lax.broadcasted_iota(jnp.int32, (16, 128), 1)
-    return jnp.where(lanes < GROUPS, average, total + count * pltpu.roll(spread, GROUPS, 1))
+    lanes = lax.broadcasted_iota(jnp.int32, (8, 128), 1)
+    is_mean = (lanes // GROUPS) % 2 == 0
+    return jnp.where(is_mean, average, total + count * pltpu.roll(spread, GROUPS, 1))
 
 
 def gather_kernel(
@@ -134,7 +135,8 @@
     mean = centre.astype(F32) + gap * (1.0 / LOCAL_COUNT)
     square = square - pltpu.roll(gap * gap, GROUPS, 1) * (1.0 / LOCAL_COUNT)
     lanes = lax.broadcasted_iota(jnp.int32, (16, 128), 1)
-    tile1[...] = jnp.where(lanes < GROUPS, mean, square)
+    tile = jnp.where(lanes < GROUPS, mean, jnp.where(lanes < 2 * GROUPS, square, 0.0))
+    tile1[...] = tile[0:8] + pltpu.roll(tile[8:16], 2 * GROUPS, 1)
 
     diagonals = (jnp.where(has_up, 1, 0) + jnp.where(has_dn, 1, 0)) * (
         jnp.where(has_lf, 1, 0) + jnp.where(has_rt, 1, 0)
@@ -200,6 +202,7 @@
     for copy in weights[:3]:
         copy.wait()
     form(wd, mid_d)
+
     for copy in weights[3:]:
         copy.wait()
     form(wl, mid_l)
@@ -235,9 +238,9 @@
 
     for copy in second:
         copy.wait_recv()
-    count = LOCAL_COUNT * NROW
-    tile = merge([tile2[...]] + [got2[d] for d in range(1, NCOL)], count)
-    count = count * NCOL
+    tile = merge([tile2[...]] + [got2[d] for d in range(1, NCOL)], LOCAL_COUNT * NROW)
+    tile = jnp.concatenate([tile, pltpu.roll(tile, 2 * GROUPS, 1)], axis=0)
+    count = LOCAL_COUNT * NROW * NCOL
     square = pltpu.roll(tile, 128 - GROUPS, 1)
 
     def everywhere(v):
@@ -261,7 +264,7 @@
     gam_l, bet_l, bia_l, gam_d, bet_d, bia_d,
     out,
     lhs_d, even, odd, sum_d, total_a, total_b, turn, scale_d, shift_d, scale_l, shift_l,
-    sem_a, sem_b,
+    sem_out,
 ):
     row = lax.axis_index("row")
     col = lax.axis_index("col")
@@ -349,7 +352,7 @@
 
     size = PAIRS * COLS
 
-    def products(get, planes, bias, n, width, total, keep, beside=None):
+    def products(get, planes, bias, n, width, total, keep, beside=None, after=None):
         at = pl.ds(n, width)
         for k in range(4):
             m = jnp.dot(get(k), planes[k, :, at], preferred_element_type=F32)
@@ -368,6 +371,8 @@
                     total[1, c] -= v
                 else:
                     keep(1, c, ct, total[1, c] - v)
+            if after is not None:
+                after(k)
 
     def keep_dilated(h, c, ct, v):
         sum_d[h, ct] = v.astype(BF16)
@@ -438,20 +443,30 @@
     products(dilated_lhs, wd, bia_d, 512, 128, total_b, keep_dilated)
     products(local_lhs, wl, bia_l, 0, 512, total_a, keep_local(total_a))
 
+    stores = []
+
+    def store(first, last, n, width):
+        at, lanes = pl.ds(8 * first, 8 * (last - first)), pl.ds(n, width)
+        copy = pltpu.make_async_copy(
+            lhs_d.at[at, :, lanes], out.at[at, :, lanes], sem_out.at[len(stores)]
+        )
+        copy.start()
+        stores.append(copy)
+
     def beside(k):
         for unit in range(3 * k, 3 * k + 3):
             blend(total_a, 0, 512, unit // 2, unit % 2)
 
-    products(local_lhs, wl, bia_l, 512, 128, total_b, keep_local(total_b), beside)
-    result = lhs_d.at[pl.ds(0, 2 * ROWS)]
-    store_a = pltpu.make_async_copy(result.at[:, :, pl.ds(0, 512)], out.at[:, :, pl.ds(0, 512)], sem_a)
-    store_a.start()
-    for unit in range(UNITS):
-        blend(total_b, 512, 128, unit // 2, unit % 2)
-    store_b = pltpu.make_async_copy(result.at[:, :, pl.ds(512, 128)], out.at[:, :, pl.ds(512, 128)], sem_b)
-    store_b.start()
-    store_a.wait()
-    store_b.wait()
+    products(
+        local_lhs, wl, bia_l, 512, 128, total_b, keep_local(total_b), beside,
+        lambda k: store(3 * k, 3 * k + 3, 0, 512),
+    )
+    for part in range(2):
+        for unit in range(6 * part, 6 * part + 6):
+            blend(total_b, 512, 128, unit // 2, unit % 2)
+        store(6 * part, 6 * part + 6, 512, 128)
+    for copy in stores:
+        copy.wait()
 
 
 VM = pl.BlockSpec(memory_space=pltpu.VMEM)
@@ -484,10 +499,10 @@
             pltpu.VMEM((COLS, ROWS), jnp.int32),
             pltpu.VMEM((KDIM, CH), BF16),
             pltpu.VMEM((KDIM, CH), BF16),
-            pltpu.VMEM((16, 128), F32),
-            pltpu.VMEM((16, 128), F32),
-            pltpu.VMEM((NROW, 16, 128), F32),
-            pltpu.VMEM((NCOL, 16, 128), F32),
+            pltpu.VMEM((8, 128), F32),
+            pltpu.VMEM((8, 128), F32),
+            pltpu.VMEM((NROW, 8, 128), F32),
+            pltpu.VMEM((NCOL, 8, 128), F32),
             dma((PARTS,)), dma, dma((6,)), dma((8,)), dma((8,)),
             dma((NROW,)), dma((NROW,)), dma((NCOL,)), dma((NCOL,)),
         ],
@@ -515,10 +530,9 @@
             pltpu.VMEM((16, CH), F32),
             pltpu.VMEM((8, CH), F32),
             pltpu.VMEM((8, CH), F32),
-            dma,
-            dma,
+            dma((6,)),
         ],
-        compiler_params=pltpu.CompilerParams(vmem_limit_bytes=26 * 2**20 + 2**18),
+        compiler_params=pltpu.CompilerParams(vmem_limit_bytes=26 * 2**20 + 2**19),
         name="conv",
     )(*gathered, *small).reshape(ROWS, COLS, CH)
 

time: 44.5 us -> 43.8 us (0.984)
  Pallas kernels: 43.5 us -> 43 us
    pallas_call x1, Pallas kernels: 19.1 us -> 18.5 us  [per_device(): pl.pallas_call(gather_kernel, out_shape=(pltpu.VMEM((UNITS + 2, STEPS + 2...]
where the time goes in v5:
time: 43.8 us; the launch traced here: 43.3 us
  Pallas kernels  43 us (98%)
    pallas_call x1, Pallas kernels, per_device(): pl.pallas_call(conv_kernel, out_shape=jax.ShapeDtypeStruct((2 * ROWS, 16,...  24.5 us
    pallas_call x1, Pallas kernels, per_device(): pl.pallas_call(gather_kernel, out_shape=(pltpu.VMEM((UNITS + 2, STEPS + 2...  18.5 us

profile of v5, /device:TPU:1, one launch (start us, length us, event | category | flops | bytes accessed | tf_op | source)
XLA Modules:
  0.0 43.3 jit_solution(3929148012500619940)
XLA Ops:
  0.0 0.0 copy-start
  0.0 0.0 copy-start.1
  0.0 0.0 copy-start.2
  0.0 0.0 copy-start.3
  0.0 0.0 copy-start.4
  0.0 0.0 copy-start.5
  0.0 18.5 %gather.1 = (bf16[14,10,16,640]{3,2,1,0:T(8,128)(2,1)S(1)}, f32[5,50,40,128]{3,2,1,0:T(8,128)S(1)}, f32[48,128]{1,0:T(8,128)S(1)}, bf16[4,1920,640]{2,1,0:T(8,12...) custom-call(bf16[48,32,640]{2,1,0:T(8,128)(2,1)} %lat_hbm.1, ...), custom_call_target="tpu_custom_call" | custom-call | tf_op jit(solution)/shard_map/gather/pallas_call | solution.py:485
  18.6 0.0 copy-done
  18.6 0.0 copy-done.1
  18.6 0.0 copy-done.2
  18.6 0.0 copy-done.3
  18.6 0.0 copy-done.4
  18.6 0.0 copy-done.5
  18.7 24.5 %conv.1 = bf16[96,16,640]{2,1,0:T(8,128)(2,1)} custom-call(bf16[14,10,16,640]{3,2,1,0:T(8,128)(2,1)S(1)} %get-tuple-element.11.xd, f32[5,50,40,128]{3,2,1,0:T(8,128)S(1)} %get-tuple-element.12.xn, f32[48,128]{1,0:T(8,128)S(1)} %get-tuple-element.13.stats, bf16[4,1920,640]{2,1,0:T(8,128)(2,1)S(1)} %get-tuple-element.14.wl, ...), custom_call_target="tpu_custom_call" | custom-call | tf_op jit(solution)/shard_map/conv/pallas_call | solution.py:516
Async XLA Ops:
  0.0 18.6 %copy-start = (f32[640]{0:T(1024)S(1)}, f32[640]{0:T(1024)}, u32[]{:S(2)}) copy-start(f32[640]{0:T(1024)} %gam_l.1) | copy-start | bytes 7684
  0.0 18.6 %copy-start.1 = (f32[640]{0:T(1024)S(1)}, f32[640]{0:T(1024)}, u32[]{:S(2)}) copy-start(f32[640]{0:T(1024)} %bet_l.1) | copy-start | bytes 7684
  0.0 18.6 %copy-start.2 = (f32[640]{0:T(1024)S(1)}, f32[640]{0:T(1024)}, u32[]{:S(2)}) copy-start(f32[640]{0:T(1024)} %bia_l.1) | copy-start | bytes 7684
  0.0 18.6 %copy-start.3 = (f32[640]{0:T(1024)S(1)}, f32[640]{0:T(1024)}, u32[]{:S(2)}) copy-start(f32[640]{0:T(1024)} %gam_d.1) | copy-start | bytes 7684
  0.0 18.6 %copy-start.4 = (f32[640]{0:T(1024)S(1)}, f32[640]{0:T(1024)}, u32[]{:S(2)}) copy-start(f32[640]{0:T(1024)} %bet_d.1) | copy-start | bytes 7684
  0.0 18.6 %copy-start.5 = (f32[640]{0:T(1024)S(1)}, f32[640]{0:T(1024)}, u32[]{:S(2)}) copy-start(f32[640]{0:T(1024)} %bia_d.1) | copy-start | bytes 7684

commit v6 on v5

--- a/solution.py
+++ b/solution.py
@@ -130,8 +130,8 @@
             copy.start()
             weights.append(copy)
 
-    gap = exact_dot(carry[0], groups_to_lanes(0))
-    square = exact_dot(carry[1], groups_to_lanes(GROUPS))
+    both = exact_dot(jnp.concatenate(carry, axis=0), groups_to_lanes(0))
+    gap, square = both[0:16], pltpu.roll(both[16:32], GROUPS, 1)
     mean = centre.astype(F32) + gap * (1.0 / LOCAL_COUNT)
     square = square - pltpu.roll(gap * gap, GROUPS, 1) * (1.0 / LOCAL_COUNT)
     lanes = lax.broadcasted_iota(jnp.int32, (16, 128), 1)
@@ -191,7 +191,7 @@
         copy.wait_recv()
     tile2[...] = merge([tile1[...]] + [got1[d] for d in range(1, NROW)], LOCAL_COUNT)
     second = []
-    for d in range(1, NCOL):
+    for d in (10, 6, 9, 7, 11, 5, 2, 14, 8, 3, 13, 1, 15, 4, 12):
         copy = pltpu.make_async_remote_copy(
             src_ref=tile2, dst_ref=got2.at[d], send_sem=send2.at[d], recv_sem=recv2.at[d],
             device_id=(row, lax.rem(col + d, NCOL)), device_id_type=MESH,

time: 43.8 us -> 43.5 us (level)
  no operation moved by 1% of the time
where the time goes in v6:
time: 43.5 us; the launch traced here: 43.1 us
  Pallas kernels  42.8 us (98%)
    pallas_call x1, Pallas kernels, per_device(): pl.pallas_call(conv_kernel, out_shape=jax.ShapeDtypeStruct((2 * ROWS, 16,...  24.5 us
    pallas_call x1, Pallas kernels, per_device(): pl.pallas_call(gather_kernel, out_shape=(pltpu.VMEM((UNITS + 2, STEPS + 2...  18.3 us

profile of v6, /device:TPU:1, one launch (start us, length us, event | category | flops | bytes accessed | tf_op | source)
XLA Modules:
  0.0 43.1 jit_solution(8624777983215050137)
XLA Ops:
  0.0 0.0 copy-start
  0.0 0.0 copy-start.1
  0.0 0.0 copy-start.2
  0.0 0.0 copy-start.3
  0.0 0.0 copy-start.4
  0.0 0.0 copy-start.5
  0.0 18.3 %gather.1 = (bf16[14,10,16,640]{3,2,1,0:T(8,128)(2,1)S(1)}, f32[5,50,40,128]{3,2,1,0:T(8,128)S(1)}, f32[48,128]{1,0:T(8,128)S(1)}, bf16[4,1920,640]{2,1,0:T(8,12...) custom-call(bf16[48,32,640]{2,1,0:T(8,128)(2,1)} %lat_hbm.1, ...), custom_call_target="tpu_custom_call" | custom-call | tf_op jit(solution)/shard_map/gather/pallas_call | solution.py:485
  18.3 0.0 copy-done
  18.3 0.0 copy-done.1
  18.4 0.0 copy-done.2
  18.4 0.0 copy-done.3
  18.4 0.0 copy-done.4
  18.4 0.0 copy-done.5
  18.4 24.5 %conv.1 = bf16[96,16,640]{2,1,0:T(8,128)(2,1)} custom-call(bf16[14,10,16,640]{3,2,1,0:T(8,128)(2,1)S(1)} %get-tuple-element.11.xd, f32[5,50,40,128]{3,2,1,0:T(8,128)S(1)} %get-tuple-element.12.xn, f32[48,128]{1,0:T(8,128)S(1)} %get-tuple-element.13.stats, bf16[4,1920,640]{2,1,0:T(8,128)(2,1)S(1)} %get-tuple-element.14.wl, ...), custom_call_target="tpu_custom_call" | custom-call | tf_op jit(solution)/shard_map/conv/pallas_call | solution.py:516
Async XLA Ops:
  0.0 18.3 %copy-start = (f32[640]{0:T(1024)S(1)}, f32[640]{0:T(1024)}, u32[]{:S(2)}) copy-start(f32[640]{0:T(1024)} %gam_l.1) | copy-start | bytes 7684
  0.0 18.3 %copy-start.1 = (f32[640]{0:T(1024)S(1)}, f32[640]{0:T(1024)}, u32[]{:S(2)}) copy-start(f32[640]{0:T(1024)} %bet_l.1) | copy-start | bytes 7684
  0.0 18.4 %copy-start.2 = (f32[640]{0:T(1024)S(1)}, f32[640]{0:T(1024)}, u32[]{:S(2)}) copy-start(f32[640]{0:T(1024)} %bia_l.1) | copy-start | bytes 7684
  0.0 18.4 %copy-start.3 = (f32[640]{0:T(1024)S(1)}, f32[640]{0:T(1024)}, u32[]{:S(2)}) copy-start(f32[640]{0:T(1024)} %gam_d.1) | copy-start | bytes 7684
  0.0 18.4 %copy-start.4 = (f32[640]{0:T(1024)S(1)}, f32[640]{0:T(1024)}, u32[]{:S(2)}) copy-start(f32[640]{0:T(1024)} %bet_d.1) | copy-start | bytes 7684
  0.0 18.4 %copy-start.5 = (f32[640]{0:T(1024)S(1)}, f32[640]{0:T(1024)}, u32[]{:S(2)}) copy-start(f32[640]{0:T(1024)} %bia_d.1) | copy-start | bytes 7684
